TPU v7x, 128 devices: a whole 4x4x4 slice. The times are simulated.
128 devices in a mesh: pp: 8 (over x_hi, z), ep: 16 (over x_lo, y, core).
Axes of the slice: x: 4 (x_hi: 2, x_lo: 2; x = x_hi * 2 + x_lo), y: 4, z: 4, core: 2. Of those that a mesh axis runs over, the one named last changes fastest.
Arguments:
- section_input: bfloat16 [8, 2048, 7168], P('pp', 'ep'), may hold values from -6 to 6
- forward_routes: int32 [8, 2048, 1], P('pp', 'ep'), may hold values from 0 to 3; in each aligned block of 128 rows (0 to 127, 128 to 255, ..., all dimensions but the last counted through in order) at most 40 rows name the same one
- forward_weight: float32 [8, 2048], P('pp', 'ep'), may hold values from 0.2 to 1
- saved_input: bfloat16 [8, 2048, 7168], P('pp', 'ep'), may hold values from -6 to 6
- section_grad: bfloat16 [8, 2048, 7168], P('pp', 'ep'), may hold values from -6 to 6
- backward_routes: int32 [8, 2048, 1], P('pp', 'ep'), may hold values from 0 to 3; in each aligned block of 128 rows (0 to 127, 128 to 255, ..., all dimensions but the last counted through in order) at most 40 rows name the same one
- backward_weight: float32 [8, 2048], P('pp', 'ep'), may hold values from 0.2 to 1
- norm_gain: bfloat16 [8, 7168], P('pp'), may hold values from 0.099609375 to 1.8984375
- w_gate: bfloat16 [8, 16, 1792, 1024], P('pp', 'ep'), may hold values from -0.0625 to 0.0625
- w_up: bfloat16 [8, 16, 1792, 1024], P('pp', 'ep'), may hold values from -0.0625 to 0.0625
- w_down: bfloat16 [8, 16, 1024, 1792], P('pp', 'ep'), may hold values from -0.1875 to 0.1875
Outputs:
- arrived_input: bfloat16 [8, 2048, 7168], P('pp', 'ep')
- arrived_grad: bfloat16 [8, 2048, 7168], P('pp', 'ep')
Inputs may be any that keep to these rules, and one draw needn't show every extreme that they name: `forward_routes`: one expert per token. In each aligned block of 128 rows (the tokens of one device) no expert is named more than 40 times, and in every draw some expert is named exactly 40 times in some block. `backward_routes`: same law as forward_routes.
All inputs are finite; a program needn't handle non-finite values.
Results may differ from a plain program's by a relative error of at most 0.0064.
Values may be sent and summed in bfloat16 or wider, within the bound.
No kernel may reach another device: no remote copies, remote signals or barrier semaphores. Data moves between devices by JAX's collectives and lax.ppermute only.
A program may use at most 192 MiB of HBM per device.

v0:
```python
import functools

import jax
import jax.numpy as jnp
from jax import lax
from jax.experimental import pallas as pl
from jax.experimental.pallas import tpu as pltpu
from jax.sharding import PartitionSpec as P

epsilon = 1e-06
VMEM_BYTES = 40 * 1024 * 1024


def from_partner(value, axis, bit):
    return lax.ppermute(value, axis, [(i, i ^ 1 << bit) for i in range(lax.axis_size(axis))])


def passed_along(value, axis, by):
    count = lax.axis_size(axis)
    return lax.ppermute(value, axis, [(i, (i + by) % count) for i in range(count)])


def exchange(value):
    return lax.all_to_all(value, "ep", split_axis=0, concat_axis=0, tiled=True)


def after(value, earlier):
    return lax.optimization_barrier((value, earlier))[0]


def contract(left, right, left_dim, right_dim):
    return lax.dot_general(
        left, right, (((left_dim,), (right_dim,)), ((), ())), preferred_element_type=jnp.float32
    )


def selections(routes, experts, capacity):
    tok_count = routes.shape[1]
    padded = 8 * pl.cdiv(experts, 8)
    named = routes == lax.broadcasted_iota(jnp.int32, (padded, tok_count), 0)
    earlier = lax.broadcasted_iota(jnp.int32, (tok_count, tok_count), 0) < lax.broadcasted_iota(
        jnp.int32, (tok_count, tok_count), 1
    )
    places = contract(
        named.astype(jnp.float32).astype(jnp.bfloat16),
        earlier.astype(jnp.float32).astype(jnp.bfloat16),
        1,
        0,
    )
    places = jnp.where(named, places, -1.0)
    slots = lax.broadcasted_iota(jnp.int32, (capacity, tok_count), 0).astype(jnp.float32)
    return [
        (places[e : e + 1, :] == slots).astype(jnp.float32).astype(jnp.bfloat16)
        for e in range(experts)
    ]


def as_column(row):
    count = row.shape[1]
    diagonal = lax.broadcasted_iota(jnp.int32, (count, count), 0) == lax.broadcasted_iota(
        jnp.int32, (count, count), 1
    )
    return jnp.sum(jnp.where(diagonal, row, 0.0), axis=1, keepdims=True)


def inverse_rms(tokens_ref, quarter):
    width = tokens_ref.shape[1]
    total = 0.0
    for q in range(width // quarter):
        values = tokens_ref[:, q * quarter : (q + 1) * quarter].astype(jnp.float32)
        total = total + jnp.sum(values * values, axis=1, keepdims=True)
    return lax.rsqrt(total * (1.0 / width) + epsilon)


def normed_kernel(routes_ref, tokens_ref, norm_ref, out_ref):
    shard_count, capacity, quarter = out_ref.shape
    experts = shard_count // 4
    picks = selections(routes_ref[...], experts, capacity)
    inv_rms = inverse_rms(tokens_ref, quarter)
    for q in range(4):
        columns = slice(q * quarter, (q + 1) * quarter)
        values = tokens_ref[:, columns].astype(jnp.float32)
        normed = (values * inv_rms * norm_ref[:, columns].astype(jnp.float32)).astype(jnp.bfloat16)
        for e in range(experts):
            out_ref[4 * e + q] = contract(picks[e], normed, 1, 0).astype(jnp.bfloat16)


def scaled_kernel(routes_ref, weight_ref, grad_ref, out_ref):
    shard_count, capacity, quarter = out_ref.shape
    experts = shard_count // 4
    picks = selections(routes_ref[...], experts, capacity)
    weight = as_column(weight_ref[...])
    for q in range(4):
        columns = slice(q * quarter, (q + 1) * quarter)
        scaled = (weight * grad_ref[:, columns].astype(jnp.float32)).astype(jnp.bfloat16)
        for e in range(experts):
            out_ref[4 * e + q] = contract(picks[e], scaled, 1, 0).astype(jnp.bfloat16)


def placed_back(picks, returned_ref, q):
    mixed = 0.0
    for e, pick in enumerate(picks):
        mixed = mixed + contract(pick, returned_ref[4 * e + q], 0, 0)
    return mixed


def forward_end_kernel(routes_ref, weight_ref, tokens_ref, returned_ref, out_ref):
    shard_count, capacity, quarter = returned_ref.shape
    picks = selections(routes_ref[...], shard_count // 4, capacity)
    weight = as_column(weight_ref[...])
    for q in range(4):
        columns = slice(q * quarter, (q + 1) * quarter)
        tokens = tokens_ref[:, columns].astype(jnp.float32)
        mixed = placed_back(picks, returned_ref, q)
        out_ref[:, columns] = (tokens + weight * mixed).astype(jnp.bfloat16)


def input_grad_kernel(widths, gate_grad_ref, up_grad_ref, rows_ref, gate_ref, up_ref, first_ref, second_ref, along_ref):
    step = pl.program_id(0)
    tile = gate_ref.shape[0]
    result = contract(gate_grad_ref[...], gate_ref[...], 1, 1)
    result = (result + contract(up_grad_ref[...], up_ref[...], 1, 1)).astype(jnp.bfloat16)
    along = jnp.sum(
        result.astype(jnp.float32) * rows_ref[...].astype(jnp.float32), axis=1, keepdims=True
    )

    @pl.when(step == 0)
    def _():
        along_ref[...] = jnp.zeros_like(along_ref)

    along_ref[...] += along
    for k in range(sum(widths) // tile):
        begin = k * tile
        target, offset = (first_ref, 0) if begin < widths[0] else (second_ref, widths[0])

        @pl.when(step == k)
        def _(target=target, begin=begin - offset):
            target[:, begin : begin + tile] = result

    @pl.when(step == pl.num_programs(0) - 1)
    def _():
        total = along_ref[...]
        high = total.astype(jnp.bfloat16)
        rest = (total - high.astype(jnp.float32)).astype(jnp.bfloat16)
        lane = lax.broadcasted_iota(jnp.int32, (total.shape[0], 128), 1)
        first_ref[:, widths[0] :] = jnp.where(
            lane == 0, high.astype(jnp.float32), jnp.where(lane == 1, rest.astype(jnp.float32), 0.0)
        ).astype(jnp.bfloat16)


def backward_first_kernel(routes_ref, tokens_ref, grad_ref, norm_ref, returned_ref, out_ref, factors_ref):
    shard_count, capacity, sent = returned_ref.shape
    width = sent - 128
    model_width = tokens_ref.shape[1]
    quarter = model_width // 4
    picks = selections(routes_ref[...], shard_count // 4, capacity)
    inv_rms = inverse_rms(tokens_ref, quarter)
    along = 0.0
    for q in range(4):
        for e, pick in enumerate(picks):
            along = along + contract(pick, returned_ref[4 * e + q, :, width:], 0, 0)
    along = jnp.sum(along, axis=1, keepdims=True)
    shrink = along * (1.0 / model_width) * inv_rms * inv_rms
    lane = lax.broadcasted_iota(jnp.int32, factors_ref.shape, 1)
    factors_ref[...] = jnp.where(lane == 0, inv_rms, shrink)
    for q in range(4):
        columns = slice(q * quarter, q * quarter + width)
        pulled = 0.0
        for e, pick in enumerate(picks):
            pulled = pulled + contract(pick, returned_ref[4 * e + q, :, :width], 0, 0)
        pulled = pulled * norm_ref[:, columns].astype(jnp.float32)
        values = tokens_ref[:, columns].astype(jnp.float32)
        own = grad_ref[:, columns].astype(jnp.float32)
        out_ref[:, q * width : (q + 1) * width] = (
            own + (pulled * inv_rms - values * shrink)
        ).astype(jnp.bfloat16)


def backward_second_kernel(routes_ref, tokens_ref, grad_ref, norm_ref, factors_ref, returned_ref, out_ref):
    shard_count, capacity, width = returned_ref.shape
    quarter = tokens_ref.shape[1] // 4
    picks = selections(routes_ref[...], shard_count // 4, capacity)
    inv_rms = factors_ref[:, 0:1]
    shrink = factors_ref[:, 1:2]
    for q in range(4):
        columns = slice((q + 1) * quarter - width, (q + 1) * quarter)
        pulled = placed_back(picks, returned_ref, q) * norm_ref[:, columns].astype(jnp.float32)
        values = tokens_ref[:, columns].astype(jnp.float32)
        own = grad_ref[:, columns].astype(jnp.float32)
        out_ref[:, q * width : (q + 1) * width] = (
            own + (pulled * inv_rms - values * shrink)
        ).astype(jnp.bfloat16)


def joined_kernel(first_ref, second_ref, out_ref):
    first = first_ref.shape[1] // 4
    second = second_ref.shape[1] // 4
    for q in range(4):
        begin = q * (first + second)
        out_ref[:, begin : begin + first] = first_ref[:, q * first : (q + 1) * first]
        out_ref[:, begin + first : begin + first + second] = second_ref[
            :, q * second : (q + 1) * second
        ]


def kernel_settings(flops, moved):
    return dict(
        compiler_params=pltpu.CompilerParams(vmem_limit_bytes=VMEM_BYTES),
        cost_estimate=pl.CostEstimate(flops=flops, bytes_accessed=moved, transcendentals=0),
    )


def local_call(kernel, shapes, *arrays):
    whole = pl.BlockSpec(memory_space=pltpu.VMEM)
    moved = sum(a.size * a.dtype.itemsize for a in arrays)
    return pl.pallas_call(
        kernel,
        out_shape=shapes,
        in_specs=[whole] * len(arrays),
        out_specs=jax.tree.map(lambda _: whole, shapes),
        **kernel_settings(1 << 28, 2 * moved),
    )(*arrays)


def input_grads(both_grads, rows, gate_w, up_w, widths, tile=256):
    row_count, hidden_width = both_grads.shape[0], gate_w.shape[1]
    steps = gate_w.shape[0] // tile
    sent = (widths[0] + 128, widths[1])
    return pl.pallas_call(
        functools.partial(input_grad_kernel, widths),
        out_shape=[jax.ShapeDtypeStruct((row_count, w), jnp.bfloat16) for w in sent],
        grid=(steps,),
        in_specs=[
            pl.BlockSpec((row_count, hidden_width), lambda i: (0, 0)),
            pl.BlockSpec((row_count, hidden_width), lambda i: (0, 1)),
            pl.BlockSpec((row_count, tile), lambda i: (0, i)),
            pl.BlockSpec((tile, hidden_width), lambda i: (i, 0)),
            pl.BlockSpec((tile, hidden_width), lambda i: (i, 0)),
        ],
        out_specs=[pl.BlockSpec((row_count, w), lambda i: (0, 0)) for w in sent],
        scratch_shapes=[pltpu.VMEM((row_count, 1), jnp.float32)],
        **kernel_settings(
            4 * row_count * hidden_width * gate_w.shape[0], 4 * gate_w.size + 4 * both_grads.size
        ),
    )(both_grads, both_grads, rows, gate_w, up_w)


def halves(rows, core):
    half = rows.shape[0] // 2
    own = lax.dynamic_slice_in_dim(rows, core * half, half, 0)
    other = lax.dynamic_slice_in_dim(rows, (1 - core) * half, half, 0)
    return own, other


def summed_over_group(own_parts, other_parts):
    sent = jnp.concatenate([part.astype(jnp.bfloat16) for part in other_parts], axis=1)
    came = from_partner(sent, "ep", 0)
    paired = jnp.concatenate(own_parts, axis=1) + came.astype(jnp.float32)
    distant = from_partner(paired.astype(jnp.bfloat16), "ep", 1)
    return paired + distant.astype(jnp.float32)


def both_halves(own, core):
    other = from_partner(own, "ep", 0)
    first = jnp.where(core == 0, own, other)
    second = jnp.where(core == 0, other, own)
    return jnp.concatenate([first, second], axis=0)


def shards(
    section_input,
    forward_routes,
    forward_weight,
    saved_input,
    section_grad,
    backward_routes,
    backward_weight,
    norm_gain,
    w_gate,
    w_up,
    w_down,
):
    experts = lax.axis_size("ep") // 4
    tok_count, model_width = section_input.shape[1:]
    capacity = tok_count * 5 // (4 * experts)
    quarter = model_width // 4
    core = lax.axis_index("ep") & 1
    gate_w = w_gate[0, 0]
    up_w = w_up[0, 0]
    down_w = w_down[0, 0]
    hidden_width = gate_w.shape[1]
    shape = (4 * experts, capacity, quarter)
    block = jax.ShapeDtypeStruct(shape, jnp.bfloat16)
    whole = jax.ShapeDtypeStruct((tok_count, model_width), jnp.bfloat16)
    widths = (quarter * 3 // 7, quarter * 4 // 7)
    fwd_tokens = section_input[0]
    fwd_routes = forward_routes.reshape(1, tok_count)
    bwd_tokens = saved_input[0]
    cotangent = section_grad[0]
    bwd_routes = backward_routes.reshape(1, tok_count)

    send_fwd = local_call(normed_kernel, block, fwd_routes, fwd_tokens, norm_gain)
    send_rows = local_call(normed_kernel, block, bwd_routes, bwd_tokens, norm_gain)
    send_grads = local_call(scaled_kernel, block, bwd_routes, backward_weight, cotangent)

    got_fwd = exchange(send_fwd)
    got_rows = exchange(after(send_rows, got_fwd))
    got_grads = exchange(after(send_grads, got_rows))

    own, other = halves(got_fwd.reshape(-1, quarter), core)
    pre = summed_over_group(
        [contract(own, gate_w, 1, 0), contract(own, up_w, 1, 0)],
        [contract(other, gate_w, 1, 0), contract(other, up_w, 1, 0)],
    )
    gate_pre = pre[:, :hidden_width]
    up_pre = pre[:, hidden_width:]
    hidden = both_halves(
        (gate_pre * jax.nn.sigmoid(gate_pre) * up_pre).astype(jnp.bfloat16), core
    )
    fwd_result = contract(hidden, down_w, 1, 0).astype(jnp.bfloat16).reshape(shape)
    fwd_returned = exchange(after(fwd_result, got_grads))

    rows = got_rows.reshape(-1, quarter)
    own, other = halves(rows, core)
    pre = summed_over_group(
        [contract(own, gate_w, 1, 0), contract(own, up_w, 1, 0)],
        [contract(other, gate_w, 1, 0), contract(other, up_w, 1, 0)],
    )
    own, other = halves(got_grads.reshape(-1, quarter), core)
    hidden_grad = summed_over_group([contract(own, down_w, 1, 1)], [contract(other, down_w, 1, 1)])
    gate_pre = pre[:, :hidden_width]
    up_pre = pre[:, hidden_width:]
    sigmoid_gate = jax.nn.sigmoid(gate_pre)
    gate_grad = (
        hidden_grad * up_pre * sigmoid_gate * (1.0 + gate_pre * (1.0 - sigmoid_gate))
    ).astype(jnp.bfloat16)
    up_grad = (hidden_grad * gate_pre * sigmoid_gate).astype(jnp.bfloat16)
    both_grads = both_halves(jnp.concatenate([gate_grad, up_grad], axis=1), core)
    both_grads, fwd_returned = lax.optimization_barrier((both_grads, fwd_returned))
    first, second = input_grads(both_grads, rows, gate_w, up_w, widths)
    first_back = exchange(first.reshape(4 * experts, capacity, -1))
    second_back = exchange(after(second, first_back).reshape(4 * experts, capacity, -1))

    layer_out = local_call(
        forward_end_kernel, whole, fwd_routes, forward_weight, fwd_tokens, fwd_returned
    )
    arrived_input = passed_along(layer_out, "pp", 1)

    first_out, factors = local_call(
        backward_first_kernel,
        [
            jax.ShapeDtypeStruct((tok_count, 4 * widths[0]), jnp.bfloat16),
            jax.ShapeDtypeStruct((tok_count, 128), jnp.float32),
        ],
        bwd_routes,
        bwd_tokens,
        cotangent,
        norm_gain,
        first_back,
    )
    second_out = local_call(
        backward_second_kernel,
        jax.ShapeDtypeStruct((tok_count, 4 * widths[1]), jnp.bfloat16),
        bwd_routes,
        bwd_tokens,
        cotangent,
        norm_gain,
        factors,
        second_back,
    )
    arrived_grad = local_call(
        joined_kernel,
        whole,
        passed_along(first_out, "pp", -1),
        passed_along(second_out, "pp", -1),
    )
    return (arrived_input[None], arrived_grad[None])


def solution(mesh):
    placed = (
        P("pp", "ep", None),
        P("pp", "ep", None),
        P("pp", "ep"),
        P("pp", "ep", None),
        P("pp", "ep", None),
        P("pp", "ep", None),
        P("pp", "ep"),
        P("pp", None),
        P("pp", "ep", None, None),
        P("pp", "ep", None, None),
        P("pp", "ep", None, None),
    )
    return jax.shard_map(
        shards,
        mesh=mesh,
        in_specs=placed,
        out_specs=(P("pp", "ep", None), P("pp", "ep", None)),
        check_vma=False,
    )
```

profile of v0, /device:TPU:1, one launch (start us, length us, event | category | flops | bytes accessed | tf_op | source)
XLA Modules:
  0.0 317.2 jit_solution(14949723839593932937)
XLA Ops:
  6.5 7.0 %all-to-all-start = ((bf16[16,40,1792]{2,1,0:T(8,128)(2,1)}), bf16[16,40,1792]{2,1,0:T(8,128)(2,1)}, u32[]{:S(2)}, u32[]{:S(2)}) async-start(bf16[16,40,1792]{2,1,0:T(8,128)(2,1)} %copy-done.5), calls=%async_computation | async-start | bytes 4587520 | tf_op jit(solution)/shard_map/all_to_all | solution.py:24
  16.6 27.1 %all-to-all-done = bf16[16,40,1792]{2,1,0:T(8,128)(2,1)} async-done(((bf16[16,40,1792]{2,1,0:T(8,128)(2,1)}), bf16[16,40,1792]{2,1,0:T(8,128)(2,1)}, u32[]{:S(2)}, u32[]{:S(2)}) %all-to-all-start) | async-done | bytes 2293792 | tf_op jit(solution)/shard_map/all_to_all | solution.py:24
  43.7 7.1 %all-to-all-start.1 = ((bf16[16,40,1792]{2,1,0:T(8,128)(2,1)}), bf16[16,40,1792]{2,1,0:T(8,128)(2,1)}, u32[]{:S(2)}, u32[]{:S(2)}) async-start(bf16[16,40,1792]{2,1,0:T(8,128)(2,1)} %copy-done.4), calls=%async_computation.1 | async-start | bytes 4587520 | tf_op jit(solution)/shard_map/all_to_all | solution.py:24
  50.9 3.9 %convolution_convert_fusion = bf16[320,1024]{1,0:T(8,128)(2,1)S(1)} fusion(bf16[640,1792]{1,0:T(8,128)(2,1)} %bitcast.10, s32[]{:T(128)S(6)} %select_n.36, bf16[1,1,1792,1024]{3,2,1,0:T(8,128)(2,1)} %param.20), kind=kOutput, calls=%fused_computation.13 | convolution fusion | flops 1174732800 | bytes 5472260 | tf_op jit(solution)/shard_map/dot_general | solution.py:32
  72.4 8.6 %all-to-all-done.1 = bf16[16,40,1792]{2,1,0:T(8,128)(2,1)} async-done(((bf16[16,40,1792]{2,1,0:T(8,128)(2,1)}), bf16[16,40,1792]{2,1,0:T(8,128)(2,1)}, u32[]{:S(2)}, u32[]{:S(2)}) %all-to-all-start.1) | async-done | bytes 2293792 | tf_op jit(solution)/shard_map/all_to_all | solution.py:24
  84.8 7.2 %all-to-all-start.2 = ((bf16[16,40,1792]{2,1,0:T(8,128)(2,1)}), bf16[16,40,1792]{2,1,0:T(8,128)(2,1)}, u32[]{:S(2)}, u32[]{:S(2)}) async-start(bf16[16,40,1792]{2,1,0:T(8,128)(2,1)} %copy-done.6), calls=%async_computation.2 | async-start | bytes 4587520 | tf_op jit(solution)/shard_map/all_to_all | solution.py:24
  92.1 3.9 %convolution_convert_fusion.3 = bf16[320,1024]{1,0:T(8,128)(2,1)S(1)} fusion(bf16[640,1792]{1,0:T(8,128)(2,1)} %bitcast.7.rows_ref, s32[]{:T(128)S(6)} %select_n.36, bf16[1,1,1792,1024]{3,2,1,0:T(8,128)(2,1)} %param.19), kind=kOutput, calls=%fused_computation.16 | convolution fusion | flops 1174732800 | bytes 5472260 | tf_op jit(solution)/shard_map/dot_general | solution.py:32
  101.2 3.9 %fusion.37 = f32[320,1024]{1,0:T(8,128)} fusion(bf16[640,1792]{1,0:T(8,128)(2,1)} %bitcast.7.rows_ref, s32[]{:T(128)S(6)} %select_n.35, bf16[1,1,1792,1024]{3,2,1,0:T(8,128)(2,1)S(1)} %copy-done.21), kind=kOutput, calls=%fused_computation.49 | convolution fusion | flops 1174405120 | bytes 6127620 | tf_op jit(solution)/shard_map/dot_general | solution.py:32
  105.1 12.6 %collective-permute-done.6 = bf16[320,2048]{1,0:T(8,128)(2,1)} collective-permute-done((bf16[320,2048]{1,0:T(8,128)(2,1)}, bf16[320,2048]{1,0:T(8,128)(2,1)}, u32[]{:S(2)}, u32[]{:S(2)}) %collective-permute-start.6) | collective-permute-done | bytes 1310752 | tf_op jit(solution)/shard_map/ppermute | solution.py:15
  122.7 12.2 %all-to-all-done.2 = bf16[16,40,1792]{2,1,0:T(8,128)(2,1)} async-done(((bf16[16,40,1792]{2,1,0:T(8,128)(2,1)}), bf16[16,40,1792]{2,1,0:T(8,128)(2,1)}, u32[]{:S(2)}, u32[]{:S(2)}) %all-to-all-start.2) | async-done | bytes 2293792 | tf_op jit(solution)/shard_map/all_to_all | solution.py:24
  134.9 3.9 %fusion.9 = bf16[320,1024]{1,0:T(8,128)(2,1)S(1)} fusion(bf16[1,1,1024,1792]{3,2,1,0:T(8,128)(2,1)} %param.21, bf16[640,1792]{1,0:T(8,128)(2,1)} %bitcast.5, s32[]{:T(128)S(6)} %select_n.36), kind=kOutput, calls=%fused_computation.12 | convolution fusion | flops 1174732800 | bytes 5472260 | tf_op jit(solution)/shard_map/dot_general | solution.py:32
  143.4 3.9 %fusion.58 = (bf16[320,1024]{1,0:T(8,128)(2,1)}, f32[320,1024]{1,0:T(8,128)}) fusion(bf16[320,1024]{1,0:T(8,128)(2,1)S(1)} %collective-permute-done, bf16[1,1,1024,1792]{3,2,1,0:T(8,128)(2,1)S(1)} %copy-done.36, bf16[640,1792]{1,0:T(8,128)(2,1)} %bitcast.5, s32[]{:T(128)S(6)} %select_n.35), kind=kOutput, calls=%fused_computation.72 | convolution fusion | flops 1175388160 | bytes 7438340 | tf_op jit(solution)/shard_map/dot_general | solution.py:32
  147.8 3.9 %fusion.6 = bf16[640,1792]{1,0:T(8,128)(2,1)} fusion(bf16[1,1,1024,1792]{3,2,1,0:T(8,128)(2,1)S(1)} %copy-done.36, bf16[320,1024]{1,0:T(8,128)(2,1)S(1)} %get-tuple-element.27, bf16[320,1024]{1,0:T(8,128)(2,1)S(1)} %get-tuple-element.26), kind=kOutput, calls=%fused_computation.6 | convolution fusion | flops 2352578560 | bytes 7274496 | tf_op jit(solution)/shard_map/dot_general | solution.py:32
  151.7 5.0 %all-to-all-start.3 = ((bf16[16,40,1792]{2,1,0:T(8,128)(2,1)}), bf16[16,40,1792]{2,1,0:T(8,128)(2,1)}, u32[]{:S(2)}, u32[]{:S(2)}) async-start(bf16[16,40,1792]{2,1,0:T(8,128)(2,1)} %bitcast.63), calls=%async_computation.3 | async-start | bytes 4587520 | tf_op jit(solution)/shard_map/all_to_all | solution.py:24
  156.8 24.5 %collective-permute-done.3 = bf16[320,2048]{1,0:T(8,128)(2,1)} collective-permute-done((bf16[320,2048]{1,0:T(8,128)(2,1)}, bf16[320,2048]{1,0:T(8,128)(2,1)}, u32[]{:S(2)}, u32[]{:S(2)}) %collective-permute-start.3) | collective-permute-done | bytes 1310752 | tf_op jit(solution)/shard_map/ppermute | solution.py:15
  184.0 13.3 %collective-permute-done.1 = bf16[320,1024]{1,0:T(8,128)(2,1)} collective-permute-done((bf16[320,1024]{1,0:T(8,128)(2,1)}, bf16[320,1024]{1,0:T(8,128)(2,1)}, u32[]{:S(2)}, u32[]{:S(2)}) %collective-permute-start.1) | collective-permute-done | bytes 655392 | tf_op jit(solution)/shard_map/ppermute | solution.py:15
  213.8 9.0 %shard_map.126 = (bf16[640,896]{1,0:T(8,128)(2,1)S(1)}, bf16[640,1024]{1,0:T(8,128)(2,1)S(1)}) custom-call(bf16[640,2048]{1,0:T(8,128)(2,1)S(1)} %copy-done.10, bf16[640,2048]{1,0:T(8,128)(2,1)S(1)} %copy-done.10, bf16[640,1792]{1,0:T(8,128)(2,1)} %bitcast.7.rows_ref, bf16[1792,1024]{1,0:T(8,128)(2,1)S(1)} %bitcast.62, bf16[1792,1024]{1,0:T(8,128)(2,1)} %bitcast.65), custom_call_target="tpu_custom_call" | custom-call | flops 4697620480 | bytes 12582912 | tf_op jit(solution)/shard_map/pallas_call | solution.py:229
  222.9 20.2 %all_to_all.30.returned_ref = bf16[16,40,896]{2,1,0:T(8,128)(2,1)} all-to-all(bf16[16,40,896]{2,1,0:T(8,128)(2,1)S(1)} %bitcast.55), channel_id=1, replica_groups=mesh['pp'=8,'ep'=16] {'ep'}, dimensions={0} | all-to-all | bytes 2293760 | tf_op jit(solution)/shard_map/all_to_all | solution.py:24
  243.1 4.2 %all-to-all-start.5 = ((bf16[16,40,1024]{2,1,0:T(8,128)(2,1)}), bf16[16,40,1024]{2,1,0:T(8,128)(2,1)S(1)}, u32[]{:S(2)}, u32[]{:S(2)}) async-start(bf16[16,40,1024]{2,1,0:T(8,128)(2,1)} %bitcast.54), calls=%async_computation.5 | async-start | bytes 2621440 | tf_op jit(solution)/shard_map/all_to_all | solution.py:24
  248.8 5.3 %shard_map.125 = bf16[128,7168]{1,0:T(8,128)(2,1)} custom-call(s32[1,128]{1,0:T(1,128)S(1)} %bitcast.61, f32[1,128]{1,0:T(1,128)S(1)} %copy-done.18, bf16[128,7168]{1,0:T(8,128)(2,1)S(1)} %bitcast.53, bf16[16,40,1792]{2,1,0:T(8,128)(2,1)} %all-to-all-done.3.returned_ref), custom_call_target="tpu_custom_call" | custom-call | flops 268435456 | bytes 8259584 | tf_op jit(solution)/shard_map/pallas_call | solution.py:216
  258.2 7.9 %all-to-all-done.5.returned_ref = bf16[16,40,1024]{2,1,0:T(8,128)(2,1)S(1)} async-done(((bf16[16,40,1024]{2,1,0:T(8,128)(2,1)}), bf16[16,40,1024]{2,1,0:T(8,128)(2,1)S(1)}, u32[]{:S(2)}, u32[]{:S(2)}) %all-to-all-start.5) | async-done | bytes 1310752 | tf_op jit(solution)/shard_map/all_to_all | solution.py:24
  269.1 6.0 %collective-permute-start.10 = (bf16[128,4096]{1,0:T(8,128)(2,1)S(1)}, bf16[128,4096]{1,0:T(8,128)(2,1)S(1)}, u32[]{:S(2)}, u32[]{:S(2)}) collective-permute-start(bf16[128,4096]{1,0:T(8,128)(2,1)S(1)} %shard_map.128), channel_id=1, source_target_pairs={{0,112},{16,0},{32,16},{48,32},{64,48},{80,64},{96,80},{112,96},{1... | collective-permute-start | bytes 3145736 | tf_op jit(solution)/shard_map/ppermute | solution.py:20
  275.2 32.8 %collective-permute-done.8 = bf16[128,7168]{1,0:T(8,128)(2,1)} collective-permute-done((bf16[128,7168]{1,0:T(8,128)(2,1)}, bf16[128,7168]{1,0:T(8,128)(2,1)}, u32[]{:S(2)}, u32[]{:S(2)}) %collective-permute-start.8) | collective-permute-done | bytes 1835040 | tf_op jit(solution)/shard_map/ppermute | solution.py:20
  307.9 5.1 %collective-permute-done.9.first_ref = bf16[128,3072]{1,0:T(8,128)(2,1)S(1)} collective-permute-done((bf16[128,3072]{1,0:T(8,128)(2,1)S(1)}, bf16[128,3072]{1,0:T(8,128)(2,1)S(1)}, u32[]{:S(2)}, u32[]{:S(2)}) %collective-permute-start.9) | collective-permute-done | bytes 786464 | tf_op jit(solution)/shard_map/ppermute | solution.py:20
  (119 shorter events, 77.4 us)
Async XLA Ops:
  6.5 7.1 %copy-start.13 = (bf16[1,7168]{1,0:T(2,128)(2,1)S(1)}, bf16[1,7168]{1,0:T(2,128)(2,1)}, u32[]{:S(2)}) copy-start(bf16[1,7168]{1,0:T(2,128)(2,1)} %norm_ref.7) | copy-start | bytes 43012
  6.5 7.1 %copy-start.14 = (s32[1,128,1]{1,2,0:T(1,128)S(1)}, s32[1,128,1]{1,2,0:T(1,128)}, u32[]{:S(2)}) copy-start(s32[1,128,1]{1,2,0:T(1,128)} %param.16) | copy-start | bytes 1540
  6.5 37.3 %all-to-all-start = ((bf16[16,40,1792]{2,1,0:T(8,128)(2,1)}), bf16[16,40,1792]{2,1,0:T(8,128)(2,1)}, u32[]{:S(2)}, u32[]{:S(2)}) async-start(bf16[16,40,1792]{2,1,0:T(8,128)(2,1)} %copy-done.5), calls=%async_computation | async-start | bytes 4587520 | tf_op jit(solution)/shard_map/all_to_all | solution.py:24
  43.7 37.3 %all-to-all-start.1 = ((bf16[16,40,1792]{2,1,0:T(8,128)(2,1)}), bf16[16,40,1792]{2,1,0:T(8,128)(2,1)}, u32[]{:S(2)}, u32[]{:S(2)}) async-start(bf16[16,40,1792]{2,1,0:T(8,128)(2,1)} %copy-done.4), calls=%async_computation.1 | async-start | bytes 4587520 | tf_op jit(solution)/shard_map/all_to_all | solution.py:24
  58.6 10.3 %collective-permute-start.5 = (bf16[320,2048]{1,0:T(8,128)(2,1)}, bf16[320,2048]{1,0:T(8,128)(2,1)S(1)}, u32[]{:S(2)}, u32[]{:S(2)}) collective-permute-start(bf16[320,2048]{1,0:T(8,128)(2,1)} %pad_maximum_fusion.3), channel_id=1, source_target_pairs={{0,1},{1,0},{2,3},{3,2},{4,5},{5,4},{6,7},{7,6},{8,9},{9,8},{10,11... | collective-permute-start | bytes 3932168 | tf_op jit(solution)/shard_map/ppermute | solution.py:15
  70.8 46.9 %collective-permute-start.6 = (bf16[320,2048]{1,0:T(8,128)(2,1)}, bf16[320,2048]{1,0:T(8,128)(2,1)}, u32[]{:S(2)}, u32[]{:S(2)}) collective-permute-start(bf16[320,2048]{1,0:T(8,128)(2,1)} %fusion.12), channel_id=1, source_target_pairs={{0,2},{1,3},{2,0},{3,1},{4,6},{5,7},{6,4},{7,5},{8,10},{9,11},{10,... | collective-permute-start | bytes 3932168 | tf_op jit(solution)/shard_map/ppermute | solution.py:15
  84.8 50.1 %all-to-all-start.2 = ((bf16[16,40,1792]{2,1,0:T(8,128)(2,1)}), bf16[16,40,1792]{2,1,0:T(8,128)(2,1)}, u32[]{:S(2)}, u32[]{:S(2)}) async-start(bf16[16,40,1792]{2,1,0:T(8,128)(2,1)} %copy-done.6), calls=%async_computation.2 | async-start | bytes 4587520 | tf_op jit(solution)/shard_map/all_to_all | solution.py:24
  97.2 41.9 %collective-permute-start.2 = (bf16[320,2048]{1,0:T(8,128)(2,1)}, bf16[320,2048]{1,0:T(8,128)(2,1)S(1)}, u32[]{:S(2)}, u32[]{:S(2)}) collective-permute-start(bf16[320,2048]{1,0:T(8,128)(2,1)} %pad_maximum_fusion.1), channel_id=1, source_target_pairs={{0,1},{1,0},{2,3},{3,2},{4,5},{5,4},{6,7},{7,6},{8,9},{9,8},{10,11... | collective-permute-start | bytes 3932168 | tf_op jit(solution)/shard_map/ppermute | solution.py:15
  101.2 16.5 %copy-start.30 = (bf16[320,2048]{1,0:T(8,128)(2,1)S(1)}, bf16[320,2048]{1,0:T(8,128)(2,1)}, u32[]{:S(2)}) copy-start(bf16[320,2048]{1,0:T(8,128)(2,1)} %copy-done.29) | copy-start | bytes 3932164
  101.2 16.5 %copy-start.32 = (f32[320,1024]{1,0:T(8,128)S(1)}, f32[320,1024]{1,0:T(8,128)}, u32[]{:S(2)}) copy-start(f32[320,1024]{1,0:T(8,128)} %copy-done.31) | copy-start | bytes 3932164
  101.2 16.5 %copy-start.34 = (f32[320,1024]{1,0:T(8,128)S(1)}, f32[320,1024]{1,0:T(8,128)}, u32[]{:S(2)}) copy-start(f32[320,1024]{1,0:T(8,128)} %copy-done.33) | copy-start | bytes 3932164
  121.4 19.3 %collective-permute-start.7 = (bf16[320,1024]{1,0:T(8,128)(2,1)}, bf16[320,1024]{1,0:T(8,128)(2,1)}, u32[]{:S(2)}, u32[]{:S(2)}) collective-permute-start(bf16[320,1024]{1,0:T(8,128)(2,1)} %fusion.14), channel_id=1, source_target_pairs={{0,1},{1,0},{2,3},{3,2},{4,5},{5,4},{6,7},{7,6},{8,9},{9,8},{10,11... | collective-permute-start | bytes 1966088 | tf_op jit(solution)/shard_map/ppermute | solution.py:15
  138.8 4.6 %collective-permute-start = (bf16[320,1024]{1,0:T(8,128)(2,1)S(1)}, bf16[320,1024]{1,0:T(8,128)(2,1)S(1)}, u32[]{:S(2)}, u32[]{:S(2)}) collective-permute-start(bf16[320,1024]{1,0:T(8,128)(2,1)S(1)} %fusion.9), channel_id=1, source_target_pairs={{0,1},{1,0},{2,3},{3,2},{4,5},{5,4},{6,7},{7,6},{8,9},{9,8},{10,11... | collective-permute-start | bytes 1966088 | tf_op jit(solution)/shard_map/ppermute | solution.py:15
  140.6 40.7 %collective-permute-start.3 = (bf16[320,2048]{1,0:T(8,128)(2,1)}, bf16[320,2048]{1,0:T(8,128)(2,1)}, u32[]{:S(2)}, u32[]{:S(2)}) collective-permute-start(bf16[320,2048]{1,0:T(8,128)(2,1)} %fusion.13), channel_id=1, source_target_pairs={{0,2},{1,3},{2,0},{3,1},{4,6},{5,7},{6,4},{7,5},{8,10},{9,11},{10,... | collective-permute-start | bytes 3932168 | tf_op jit(solution)/shard_map/ppermute | solution.py:15
  147.3 50.0 %collective-permute-start.1 = (bf16[320,1024]{1,0:T(8,128)(2,1)}, bf16[320,1024]{1,0:T(8,128)(2,1)}, u32[]{:S(2)}, u32[]{:S(2)}) collective-permute-start(bf16[320,1024]{1,0:T(8,128)(2,1)} %get-tuple-element.28), channel_id=1, source_target_pairs={{0,2},{1,3},{2,0},{3,1},{4,6},{5,7},{6,4},{7,5},{8,10},{9,11},{10,... | collective-permute-start | bytes 1966088 | tf_op jit(solution)/shard_map/ppermute | solution.py:15
  151.7 58.3 %all-to-all-start.3 = ((bf16[16,40,1792]{2,1,0:T(8,128)(2,1)}), bf16[16,40,1792]{2,1,0:T(8,128)(2,1)}, u32[]{:S(2)}, u32[]{:S(2)}) async-start(bf16[16,40,1792]{2,1,0:T(8,128)(2,1)} %bitcast.63), calls=%async_computation.3 | async-start | bytes 4587520 | tf_op jit(solution)/shard_map/all_to_all | solution.py:24
  156.8 40.6 %copy-start.35 = (f32[320,1024]{1,0:T(8,128)S(1)}, f32[320,1024]{1,0:T(8,128)}, u32[]{:S(2)}) copy-start(f32[320,1024]{1,0:T(8,128)} %get-tuple-element.29) | copy-start | bytes 3932164
  199.2 4.8 %collective-permute-start.4 = (bf16[320,2048]{1,0:T(8,128)(2,1)S(1)}, bf16[320,2048]{1,0:T(8,128)(2,1)S(1)}, u32[]{:S(2)}, u32[]{:S(2)}) collective-permute-start(bf16[320,2048]{1,0:T(8,128)(2,1)S(1)} %pad_maximum_fusion.2), channel_id=1, source_target_pairs={{0,1},{1,0},{2,3},{3,2},{4,5},{5,4},{6,7},{7,6},{8,9},{9,8},{10,11... | collective-permute-start | bytes 3932168 | tf_op jit(solution)/shard_map/ppermute | solution.py:15
  222.9 20.2 %copy-start.11 = (bf16[640,1024]{1,0:T(8,128)(2,1)}, bf16[640,1024]{1,0:T(8,128)(2,1)S(1)}, u32[]{:S(2)}) copy-start(bf16[640,1024]{1,0:T(8,128)(2,1)S(1)} %get-tuple-element.21) | copy-start | bytes 3932164
  243.1 23.0 %all-to-all-start.5 = ((bf16[16,40,1024]{2,1,0:T(8,128)(2,1)}), bf16[16,40,1024]{2,1,0:T(8,128)(2,1)S(1)}, u32[]{:S(2)}, u32[]{:S(2)}) async-start(bf16[16,40,1024]{2,1,0:T(8,128)(2,1)} %bitcast.54), calls=%async_computation.5 | async-start | bytes 2621440 | tf_op jit(solution)/shard_map/all_to_all | solution.py:24
  254.1 53.8 %collective-permute-start.8 = (bf16[128,7168]{1,0:T(8,128)(2,1)}, bf16[128,7168]{1,0:T(8,128)(2,1)}, u32[]{:S(2)}, u32[]{:S(2)}) collective-permute-start(bf16[128,7168]{1,0:T(8,128)(2,1)} %shard_map.125), channel_id=1, source_target_pairs={{0,16},{16,32},{32,48},{48,64},{64,80},{80,96},{96,112},{112,0},{1... | collective-permute-start | bytes 5505032 | tf_op jit(solution)/shard_map/ppermute | solution.py:20
  267.6 7.5 %copy-start.24 = (bf16[128,3072]{1,0:T(8,128)(2,1)S(1)}, bf16[128,3072]{1,0:T(8,128)(2,1)}, u32[]{:S(2)}) copy-start(bf16[128,3072]{1,0:T(8,128)(2,1)} %copy-done.23) | copy-start | bytes 2359300
  269.1 44.0 %collective-permute-start.10 = (bf16[128,4096]{1,0:T(8,128)(2,1)S(1)}, bf16[128,4096]{1,0:T(8,128)(2,1)S(1)}, u32[]{:S(2)}, u32[]{:S(2)}) collective-permute-start(bf16[128,4096]{1,0:T(8,128)(2,1)S(1)} %shard_map.128), channel_id=1, source_target_pairs={{0,112},{16,0},{32,16},{48,32},{64,48},{80,64},{96,80},{112,96},{1... | collective-permute-start | bytes 3145736 | tf_op jit(solution)/shard_map/ppermute | solution.py:20
  275.1 38.0 %collective-permute-start.9 = (bf16[128,3072]{1,0:T(8,128)(2,1)S(1)}, bf16[128,3072]{1,0:T(8,128)(2,1)S(1)}, u32[]{:S(2)}, u32[]{:S(2)}) collective-permute-start(bf16[128,3072]{1,0:T(8,128)(2,1)S(1)} %copy-done.24), channel_id=1, source_target_pairs={{0,112},{16,0},{32,16},{48,32},{64,48},{80,64},{96,80},{112,96},{1... | collective-permute-start | bytes 2359304 | tf_op jit(solution)/shard_map/ppermute | solution.py:20
  (31 other events, 89.6 us)
where the time goes:
time: 319 us; the launch traced here: 317 us
  waiting for transfers between devices  150 us (47%)
  starting transfers between devices  44.5 us (14%)
  matrix products  40.2 us (13%)
  Pallas kernels  23 us (7%)
  blocking collectives  20.2 us (6%)
  local copies, waits for them, and re-layouts  19.6 us (6%)
  other arithmetic  18.2 us (6%)
    all_to_all x5, waiting for transfers between devices, exchange(): return lax.all_to_all(value, 'ep', split_axis=0, concat_axis=0, tiled=True)  59.4 us
    ppermute x8, waiting for transfers between devices, from_partner(): lax.ppermute(value, axis, [(i, i ^ 1 << bit) for i in range(lax.axis_size...  53.1 us
    dot_general x11, matrix products, contract(): lax.dot_general(left, right, (((left_dim,), (right_dim,)), ((), ())), pre...  40.2 us
    ppermute x3, waiting for transfers between devices, passed_along(): lax.ppermute(value, axis, [(i, (i + by) % count) for i in range(count)])  37.8 us
    all_to_all x5, starting transfers between devices, exchange(): return lax.all_to_all(value, 'ep', split_axis=0, concat_axis=0, tiled=True)  30.7 us
    all_to_all x1, blocking collectives, exchange(): return lax.all_to_all(value, 'ep', split_axis=0, concat_axis=0, tiled=True)  20.2 us
    unnamed x79, local copies, waits for them, and re-layouts  19.6 us
    pallas_call x7, Pallas kernels, local_call(): pl.pallas_call(kernel, out_shape=shapes, in_specs=[whole] * len(arrays),...  14 us
  transfers between devices with their start and end apart: 16, of which 11 were waited for; matrix products, arithmetic and copies ran while one was open for 18% of the time, Pallas kernels for 4%

commit v1 on v0

v1 whole, which is shorter than its diff:
```python
import functools

import jax
import jax.numpy as jnp
from jax import lax
from jax.experimental import pallas as pl
from jax.experimental.pallas import tpu as pltpu
from jax.sharding import PartitionSpec as P

epsilon = 1e-06
VMEM_BYTES = 60 * 1024 * 1024
LOCAL_VMEM_BYTES = 36 * 1024 * 1024


def from_partner(value, axis, bit):
    return lax.ppermute(value, axis, [(i, i ^ 1 << bit) for i in range(lax.axis_size(axis))])


def passed_along(value, axis, by):
    count = lax.axis_size(axis)
    return lax.ppermute(value, axis, [(i, (i + by) % count) for i in range(count)])


def exchange(value):
    return lax.all_to_all(value, "ep", split_axis=0, concat_axis=0, tiled=True)


def after(value, earlier):
    return lax.optimization_barrier((value, earlier))[0]


def contract(left, right, left_dim, right_dim):
    return lax.dot_general(
        left, right, (((left_dim,), (right_dim,)), ((), ())), preferred_element_type=jnp.float32
    )


def selections(routes, experts, capacity):
    tok_count = routes.shape[1]
    padded = 8 * pl.cdiv(experts, 8)
    named = routes == lax.broadcasted_iota(jnp.int32, (padded, tok_count), 0)
    earlier = lax.broadcasted_iota(jnp.int32, (tok_count, tok_count), 0) < lax.broadcasted_iota(
        jnp.int32, (tok_count, tok_count), 1
    )
    places = contract(
        named.astype(jnp.float32).astype(jnp.bfloat16),
        earlier.astype(jnp.float32).astype(jnp.bfloat16),
        1,
        0,
    )
    places = jnp.where(named, places, -1.0)
    slots = lax.broadcasted_iota(jnp.int32, (capacity, tok_count), 0).astype(jnp.float32)
    return [
        (places[e : e + 1, :] == slots).astype(jnp.float32).astype(jnp.bfloat16)
        for e in range(experts)
    ]


def as_column(row):
    count = row.shape[1]
    diagonal = lax.broadcasted_iota(jnp.int32, (count, count), 0) == lax.broadcasted_iota(
        jnp.int32, (count, count), 1
    )
    return jnp.sum(jnp.where(diagonal, row, 0.0), axis=1, keepdims=True)


def inverse_rms(tokens_ref, quarter):
    width = tokens_ref.shape[1]
    total = 0.0
    for q in range(width // quarter):
        values = tokens_ref[:, q * quarter : (q + 1) * quarter].astype(jnp.float32)
        total = total + jnp.sum(values * values, axis=1, keepdims=True)
    return lax.rsqrt(total * (1.0 / width) + epsilon)


def normed_kernel(routes_ref, tokens_ref, norm_ref, out_ref, picks_ref, inv_rms_ref):
    experts, _, capacity, quarter = out_ref.shape
    q = pl.program_id(0)

    @pl.when(q == 0)
    def _():
        for e, pick in enumerate(selections(routes_ref[...], experts, capacity)):
            picks_ref[e] = pick
        inv_rms_ref[...] = inverse_rms(tokens_ref, quarter)

    columns = pl.ds(pl.multiple_of(q * quarter, 128), quarter)
    values = tokens_ref[:, columns].astype(jnp.float32)
    norm = norm_ref[:, columns].astype(jnp.float32)
    normed = (values * inv_rms_ref[...] * norm).astype(jnp.bfloat16)
    for e in range(experts):
        out_ref[e, 0] = contract(picks_ref[e], normed, 1, 0).astype(jnp.bfloat16)


def scaled_kernel(routes_ref, weight_ref, grad_ref, out_ref):
    experts, _, capacity, _ = out_ref.shape
    picks = selections(routes_ref[...], experts, capacity)
    weight = as_column(weight_ref[...])
    scaled = (weight * grad_ref[...].astype(jnp.float32)).astype(jnp.bfloat16)
    for e in range(experts):
        out_ref[e, 0] = contract(picks[e], scaled, 1, 0).astype(jnp.bfloat16)


def to_experts(kernel, arrays, specs, experts, capacity, quarter, scratch=()):
    sent = pl.pallas_call(
        kernel,
        out_shape=jax.ShapeDtypeStruct((experts, 4, capacity, quarter), jnp.bfloat16),
        grid=(4,),
        in_specs=specs,
        out_specs=pl.BlockSpec((experts, 1, capacity, quarter), lambda q: (0, q, 0, 0)),
        scratch_shapes=list(scratch),
        **kernel_settings(1 << 29, 1 << 23),
    )(*arrays)
    return sent.reshape(experts * 4, capacity, quarter)


def whole_block(array):
    return pl.BlockSpec(array.shape, lambda *_: (0,) * array.ndim)


def normed_to_experts(routes, tokens, norm, experts, capacity):
    tok_count, width = tokens.shape
    return to_experts(
        normed_kernel,
        (routes, tokens, norm),
        [whole_block(routes), whole_block(tokens), whole_block(norm)],
        experts,
        capacity,
        width // 4,
        [
            pltpu.VMEM((experts, capacity, tok_count), jnp.bfloat16),
            pltpu.VMEM((tok_count, 1), jnp.float32),
        ],
    )


def scaled_to_experts(routes, weight, grads, experts, capacity):
    tok_count, width = grads.shape
    return to_experts(
        scaled_kernel,
        (routes, weight, grads),
        [
            whole_block(routes),
            whole_block(weight),
            pl.BlockSpec((tok_count, width // 4), lambda q: (0, q)),
        ],
        experts,
        capacity,
        width // 4,
    )


def placed_back(picks, returned_ref, q):
    mixed = 0.0
    for e, pick in enumerate(picks):
        mixed = mixed + contract(pick, returned_ref[4 * e + q], 0, 0)
    return mixed


def forward_end_kernel(routes_ref, weight_ref, tokens_ref, returned_ref, out_ref):
    shard_count, capacity, quarter = returned_ref.shape
    picks = selections(routes_ref[...], shard_count // 4, capacity)
    weight = as_column(weight_ref[...])
    for q in range(4):
        columns = slice(q * quarter, (q + 1) * quarter)
        tokens = tokens_ref[:, columns].astype(jnp.float32)
        mixed = placed_back(picks, returned_ref, q)
        out_ref[:, columns] = (tokens + weight * mixed).astype(jnp.bfloat16)


def backward_first_kernel(routes_ref, tokens_ref, grad_ref, norm_ref, returned_ref, out_ref, factors_ref):
    shard_count, capacity, sent = returned_ref.shape
    width = sent - 128
    model_width = tokens_ref.shape[1]
    quarter = model_width // 4
    picks = selections(routes_ref[...], shard_count // 4, capacity)
    inv_rms = inverse_rms(tokens_ref, quarter)
    along = 0.0
    for q in range(4):
        for e, pick in enumerate(picks):
            along = along + contract(pick, returned_ref[4 * e + q, :, width:], 0, 0)
    along = 0.25 * jnp.sum(along, axis=1, keepdims=True)
    shrink = along * (1.0 / model_width) * inv_rms * inv_rms
    lane = lax.broadcasted_iota(jnp.int32, factors_ref.shape, 1)
    factors_ref[...] = jnp.where(lane == 0, inv_rms, shrink)
    for q in range(4):
        columns = slice(q * quarter, q * quarter + width)
        pulled = 0.0
        for e, pick in enumerate(picks):
            pulled = pulled + contract(pick, returned_ref[4 * e + q, :, :width], 0, 0)
        pulled = pulled * norm_ref[:, columns].astype(jnp.float32)
        values = tokens_ref[:, columns].astype(jnp.float32)
        own = grad_ref[:, columns].astype(jnp.float32)
        out_ref[:, q * width : (q + 1) * width] = (
            own + (pulled * inv_rms - values * shrink)
        ).astype(jnp.bfloat16)


def backward_second_kernel(routes_ref, tokens_ref, grad_ref, norm_ref, factors_ref, returned_ref, out_ref):
    shard_count, capacity, width = returned_ref.shape
    quarter = tokens_ref.shape[1] // 4
    picks = selections(routes_ref[...], shard_count // 4, capacity)
    inv_rms = factors_ref[:, 0:1]
    shrink = factors_ref[:, 1:2]
    for q in range(4):
        columns = slice((q + 1) * quarter - width, (q + 1) * quarter)
        pulled = placed_back(picks, returned_ref, q) * norm_ref[:, columns].astype(jnp.float32)
        values = tokens_ref[:, columns].astype(jnp.float32)
        own = grad_ref[:, columns].astype(jnp.float32)
        out_ref[:, q * width : (q + 1) * width] = (
            own + (pulled * inv_rms - values * shrink)
        ).astype(jnp.bfloat16)


def copy_kernel(piece_ref, out_ref):
    out_ref[...] = piece_ref[...]


def joined_kernel(first_ref, second_ref, out_ref):
    first = first_ref.shape[1] // 4
    second = second_ref.shape[1] // 4
    for q in range(4):
        begin = q * (first + second)
        out_ref[:, begin : begin + first] = first_ref[:, q * first : (q + 1) * first]
        out_ref[:, begin + first : begin + first + second] = second_ref[
            :, q * second : (q + 1) * second
        ]


def kernel_settings(flops, moved, vmem=VMEM_BYTES):
    return dict(
        compiler_params=pltpu.CompilerParams(vmem_limit_bytes=vmem),
        cost_estimate=pl.CostEstimate(flops=flops, bytes_accessed=moved, transcendentals=0),
    )


def local_call(kernel, shapes, *arrays, flops=1 << 28):
    whole = pl.BlockSpec(memory_space=pltpu.VMEM)
    return pl.pallas_call(
        kernel,
        out_shape=shapes,
        in_specs=[whole] * len(arrays),
        out_specs=jax.tree.map(lambda _: whole, shapes),
        **kernel_settings(flops, 1 << 22, LOCAL_VMEM_BYTES),
    )(*arrays)


def paired_product(rows, weight, weight_dim, core):
    product = contract(rows, weight, 1, weight_dim).astype(jnp.bfloat16)
    product = product.reshape(2, -1, product.shape[1])
    product = lax.optimization_barrier(product)
    own = lax.dynamic_index_in_dim(product, core, 0, keepdims=False)
    other = lax.dynamic_index_in_dim(product, 1 - core, 0, keepdims=False)
    came = from_partner(other, "ep", 0)
    return (own.astype(jnp.float32) + came.astype(jnp.float32)).astype(jnp.bfloat16)


def both_halves(own, core, earlier=()):
    other = after(from_partner(own, "ep", 0), earlier)
    first = jnp.where(core == 0, own, other)
    second = jnp.where(core == 0, other, own)
    return jnp.concatenate([first, second], axis=0)


def whole_sum(paired, distant):
    return paired.astype(jnp.float32) + distant.astype(jnp.float32)


def shards(
    section_input,
    forward_routes,
    forward_weight,
    saved_input,
    section_grad,
    backward_routes,
    backward_weight,
    norm_gain,
    w_gate,
    w_up,
    w_down,
):
    experts = lax.axis_size("ep") // 4
    tok_count, model_width = section_input.shape[1:]
    capacity = tok_count * 5 // (4 * experts)
    quarter = model_width // 4
    core = (lax.axis_index("ep") & 1)
    gate_w = w_gate[0, 0]
    up_w = w_up[0, 0]
    down_w = w_down[0, 0]
    hidden_width = gate_w.shape[1]
    shape = (4 * experts, capacity, quarter)
    whole = jax.ShapeDtypeStruct((tok_count, model_width), jnp.bfloat16)
    widths = (quarter * 3 // 7, quarter * 4 // 7)
    fwd_tokens = section_input[0]
    fwd_routes = forward_routes.reshape(1, tok_count)
    bwd_tokens = saved_input[0]
    cotangent = section_grad[0]
    bwd_routes = backward_routes.reshape(1, tok_count)

    send_fwd = normed_to_experts(fwd_routes, fwd_tokens, norm_gain, experts, capacity)
    send_rows = normed_to_experts(bwd_routes, bwd_tokens, norm_gain, experts, capacity)
    send_grads = scaled_to_experts(bwd_routes, backward_weight, cotangent, experts, capacity)

    got_fwd = exchange(send_fwd)
    got_rows = exchange(after(send_rows, got_fwd))

    fwd_rows = got_fwd.reshape(-1, quarter)
    bwd_rows = got_rows.reshape(-1, quarter)

    fwd_gate = paired_product(fwd_rows, gate_w, 0, core)
    fwd_gate_distant = from_partner(fwd_gate, "ep", 1)
    fwd_up = paired_product(fwd_rows, up_w, 0, core)
    fwd_up_distant = from_partner(fwd_up, "ep", 1)

    got_grads = exchange(after(send_grads, (got_rows, fwd_gate, fwd_up)))
    grad_rows = got_grads.reshape(-1, quarter)
    bwd_gate = paired_product(after(bwd_rows, fwd_gate_distant), gate_w, 0, core)
    bwd_gate_distant = from_partner(bwd_gate, "ep", 1)
    bwd_up = paired_product(after(bwd_rows, fwd_up_distant), up_w, 0, core)
    bwd_up_distant = from_partner(bwd_up, "ep", 1)

    gate_pre = whole_sum(fwd_gate, after(fwd_gate_distant, (bwd_gate, bwd_up)))
    up_pre = whole_sum(fwd_up, fwd_up_distant)
    hidden = both_halves(
        (gate_pre * jax.nn.sigmoid(gate_pre) * up_pre).astype(jnp.bfloat16), core
    )
    fwd_result = contract(hidden, down_w, 1, 0).astype(jnp.bfloat16)
    fwd_returned = exchange(after(fwd_result, got_grads).reshape(shape))

    hidden_grad = paired_product(after(grad_rows, bwd_gate_distant), down_w, 1, core)
    hidden_grad_distant = from_partner(after(hidden_grad, (bwd_up_distant, fwd_result)), "ep", 1)
    gate_pre = whole_sum(bwd_gate, bwd_gate_distant)
    up_pre = whole_sum(bwd_up, bwd_up_distant)
    hidden_grad = whole_sum(hidden_grad, hidden_grad_distant)
    sigmoid_gate = jax.nn.sigmoid(gate_pre)
    gate_grad = hidden_grad * up_pre * sigmoid_gate * (1.0 + gate_pre * (1.0 - sigmoid_gate))
    up_grad = hidden_grad * gate_pre * sigmoid_gate
    along = jnp.sum(gate_grad * gate_pre + up_grad * up_pre, axis=1, keepdims=True)
    high = lax.reduce_precision(along, 8, 7)
    lane = lax.broadcasted_iota(jnp.int32, (along.shape[0], 128), 1)
    along = jnp.where(lane == 0, high, jnp.where(lane == 1, along - high, 0.0))
    grads = jnp.concatenate([gate_grad, up_grad, along], axis=1).astype(jnp.bfloat16)
    grads = both_halves(grads, core, fwd_returned)
    gate_grad = grads[:, :hidden_width]
    up_grad = grads[:, hidden_width : 2 * hidden_width]
    along = grads[:, 2 * hidden_width :]

    def input_grads(begin, end):
        result = contract(gate_grad, gate_w[begin:end], 1, 1)
        return (result + contract(up_grad, up_w[begin:end], 1, 1)).astype(jnp.bfloat16)

    first = jnp.concatenate([input_grads(0, widths[0]), along], axis=1)
    first_back = exchange(first.reshape(4 * experts, capacity, -1))
    second = input_grads(widths[0], quarter)

    layer_out = local_call(
        forward_end_kernel, whole, fwd_routes, forward_weight, fwd_tokens, fwd_returned
    )
    arrived_input = passed_along(after(layer_out, first_back), "pp", 1)

    second = after(second, (first_back, layer_out))
    second_back = exchange(second.reshape(4 * experts, capacity, -1))
    first_out, factors = local_call(
        backward_first_kernel,
        [
            jax.ShapeDtypeStruct((tok_count, 4 * widths[0]), jnp.bfloat16),
            jax.ShapeDtypeStruct((tok_count, 128), jnp.float32),
        ],
        bwd_routes,
        bwd_tokens,
        cotangent,
        norm_gain,
        first_back,
    )
    second_out = local_call(
        backward_second_kernel,
        jax.ShapeDtypeStruct((tok_count, 4 * widths[1]), jnp.bfloat16),
        bwd_routes,
        bwd_tokens,
        cotangent,
        norm_gain,
        factors,
        second_back,
    )
    arrived_input = local_call(copy_kernel, whole, after(arrived_input, second_out))
    first_out = passed_along(first_out, "pp", -1)
    first_out = local_call(
        copy_kernel, jax.ShapeDtypeStruct(first_out.shape, jnp.bfloat16), first_out, flops=1 << 40
    )
    second_out = passed_along(second_out, "pp", -1)
    arrived_grad = local_call(joined_kernel, whole, first_out, second_out)
    return (arrived_input[None], arrived_grad[None])


def solution(mesh):
    specs = (
        P("pp", "ep", None),
        P("pp", "ep", None),
        P("pp", "ep"),
        P("pp", "ep", None),
        P("pp", "ep", None),
        P("pp", "ep", None),
        P("pp", "ep"),
        P("pp", None),
        P("pp", "ep", None, None),
        P("pp", "ep", None, None),
        P("pp", "ep", None, None),
    )
    return jax.shard_map(
        shards,
        mesh=mesh,
        in_specs=specs,
        out_specs=(P("pp", "ep", None), P("pp", "ep", None)),
        check_vma=False,
    )
```

time: 319 us -> 309 us (0.969)
  blocking collectives: 20.2 us -> 0 us
  starting transfers between devices: 44.5 us -> 61.6 us
  local copies, waits for them, and re-layouts: 19.6 us -> 8.61 us
  other arithmetic: 18.2 us -> 10.9 us
  Pallas kernels: 23 us -> 30.1 us
  waiting for transfers between devices: 150 us -> 155 us
    ppermute x8 -> x12, waiting for transfers between devices: 53.1 us -> 77.5 us  [from_partner(): lax.ppermute(value, axis, [(i, i ^ 1 << bit) for i in range(lax.axis_size...]
    all_to_all x1 -> x0, blocking collectives: 20.2 us -> none  [exchange(): return lax.all_to_all(value, 'ep', split_axis=0, concat_axis=0, tiled=True)]
    all_to_all x5 -> x6, waiting for transfers between devices: 59.4 us -> 47.3 us  [exchange(): return lax.all_to_all(value, 'ep', split_axis=0, concat_axis=0, tiled=True)]
    ppermute x8 -> x12, starting transfers between devices: 6.14 us -> 18 us  [from_partner(): lax.ppermute(value, axis, [(i, i ^ 1 << bit) for i in range(lax.axis_size...]
    unnamed x79 -> x60, local copies, waits for them, and re-layouts: 19.6 us -> 8.36 us
    ppermute x3, waiting for transfers between devices: 37.8 us -> 30.7 us  [passed_along(): lax.ppermute(value, axis, [(i, (i + by) % count) for i in range(count)])]
    pallas_call x1 -> x3, Pallas kernels: 9.01 us -> 15 us  [to_experts(): pl.pallas_call(kernel, out_shape=jax.ShapeDtypeStruct((experts, 4, capaci...]
    add x2 -> x0, other arithmetic: 4.68 us -> none  [summed_over_group(): return paired + distant.astype(jnp.float32)]
  transfers between devices with their start and end apart: 16 -> 21, of which waited for: 11 -> 13; matrix products, arithmetic and copies ran while one was open for 18% -> 14% of each run, Pallas kernels for 4% -> 7%
where the time goes in v1:
time: 309 us; the launch traced here: 308 us
  waiting for transfers between devices  155 us (50%)
  starting transfers between devices  61.6 us (20%)
  matrix products  39.8 us (13%)
  Pallas kernels  30.1 us (10%)
  other arithmetic  10.9 us (4%)
  local copies, waits for them, and re-layouts  8.61 us (3%)
    ppermute x12, waiting for transfers between devices, from_partner(): lax.ppermute(value, axis, [(i, i ^ 1 << bit) for i in range(lax.axis_size...  77.5 us
    all_to_all x6, waiting for transfers between devices, exchange(): return lax.all_to_all(value, 'ep', split_axis=0, concat_axis=0, tiled=True)  47.3 us
    dot_general x10, matrix products, contract(): lax.dot_general(left, right, (((left_dim,), (right_dim,)), ((), ())), pre...  39.8 us
    all_to_all x6, starting transfers between devices, exchange(): return lax.all_to_all(value, 'ep', split_axis=0, concat_axis=0, tiled=True)  31.6 us
    ppermute x3, waiting for transfers between devices, passed_along(): lax.ppermute(value, axis, [(i, (i + by) % count) for i in range(count)])  30.7 us
    ppermute x12, starting transfers between devices, from_partner(): lax.ppermute(value, axis, [(i, i ^ 1 << bit) for i in range(lax.axis_size...  18 us
    pallas_call x6, Pallas kernels, local_call(): pl.pallas_call(kernel, out_shape=shapes, in_specs=[whole] * len(arrays),...  15 us
    pallas_call x3, Pallas kernels, to_experts(): pl.pallas_call(kernel, out_shape=jax.ShapeDtypeStruct((experts, 4, capaci...  15 us
  transfers between devices with their start and end apart: 21, of which 13 were waited for; matrix products, arithmetic and copies ran while one was open for 14% of the time, Pallas kernels for 7%

profile of v1, /device:TPU:1, one launch (start us, length us, event | category | flops | bytes accessed | tf_op | source)
XLA Modules:
  0.0 307.5 jit_solution(7319387325427945626)
XLA Ops:
  0.6 5.1 %shard_map.122 = bf16[4,4,40,1792]{3,2,1,0:T(8,128)(2,1)} custom-call(s32[1,128]{1,0:T(1,128)} %bitcast.106, bf16[128,7168]{1,0:T(8,128)(2,1)} %bitcast.100, bf16[1,7168]{1,0:T(2,128)(2,1)} %norm_ref.7), custom_call_target="tpu_custom_call" | custom-call | flops 536870912 | bytes 8388608 | tf_op jit(solution)/shard_map/pallas_call | solution.py:104
  5.7 6.9 %all-to-all-start = ((bf16[16,40,1792]{2,1,0:T(8,128)(2,1)}), bf16[16,40,1792]{2,1,0:T(8,128)(2,1)S(1)}, u32[]{:S(2)}, u32[]{:S(2)}) async-start(bf16[16,40,1792]{2,1,0:T(8,128)(2,1)} %bitcast.109), calls=%async_computation | async-start | bytes 4587520 | tf_op jit(solution)/shard_map/all_to_all | solution.py:25
  12.6 5.1 %shard_map.123 = bf16[4,4,40,1792]{3,2,1,0:T(8,128)(2,1)} custom-call(s32[1,128]{1,0:T(1,128)} %bitcast.102, bf16[128,7168]{1,0:T(8,128)(2,1)} %bitcast.94, bf16[1,7168]{1,0:T(2,128)(2,1)} %norm_ref.7), custom_call_target="tpu_custom_call" | custom-call | flops 536870912 | bytes 8388608 | tf_op jit(solution)/shard_map/pallas_call | solution.py:104
  17.7 25.0 %all-to-all-done = bf16[16,40,1792]{2,1,0:T(8,128)(2,1)S(1)} async-done(((bf16[16,40,1792]{2,1,0:T(8,128)(2,1)}), bf16[16,40,1792]{2,1,0:T(8,128)(2,1)S(1)}, u32[]{:S(2)}, u32[]{:S(2)}) %all-to-all-start) | async-done | bytes 2293792 | tf_op jit(solution)/shard_map/all_to_all | solution.py:25
  42.7 7.1 %all-to-all-start.1 = ((bf16[16,40,1792]{2,1,0:T(8,128)(2,1)}), bf16[16,40,1792]{2,1,0:T(8,128)(2,1)}, u32[]{:S(2)}, u32[]{:S(2)}) async-start(bf16[16,40,1792]{2,1,0:T(8,128)(2,1)} %bitcast.108), calls=%async_computation.1 | async-start | bytes 4587520 | tf_op jit(solution)/shard_map/all_to_all | solution.py:25
  49.9 4.7 %fusion.23 = bf16[640,1024]{1,0:T(8,128)(2,1)S(1)} fusion(bf16[640,1792]{1,0:T(8,128)(2,1)S(1)} %bitcast.112, bf16[1,1,1792,1024]{3,2,1,0:T(8,128)(2,1)} %param.19), kind=kOutput, calls=%fused_computation.28 | convolution fusion | flops 2349465600 | bytes 7274496 | tf_op jit(solution)/shard_map/dot_general | solution.py:33
  60.1 4.8 %shard_map.124 = bf16[4,4,40,1792]{3,2,1,0:T(8,128)(2,1)} custom-call(s32[1,128]{1,0:T(1,128)} %bitcast.103, f32[1,128]{1,0:T(1,128)} %weight_ref.2, bf16[128,7168]{1,0:T(8,128)(2,1)} %bitcast.97), custom_call_target="tpu_custom_call" | custom-call | flops 536870912 | bytes 8388608 | tf_op jit(solution)/shard_map/pallas_call | solution.py:104
  65.3 28.1 %collective-permute-done.1 = bf16[320,1024]{1,0:T(8,128)(2,1)} collective-permute-done((bf16[320,1024]{1,0:T(8,128)(2,1)S(1)}, bf16[320,1024]{1,0:T(8,128)(2,1)}, u32[]{:S(2)}, u32[]{:S(2)}) %collective-permute-start.1) | collective-permute-done | bytes 655392 | tf_op jit(solution)/shard_map/ppermute | solution.py:16
  93.5 5.3 %fusion.26 = bf16[640,1024]{1,0:T(8,128)(2,1)S(1)} fusion(bf16[640,1792]{1,0:T(8,128)(2,1)} %bitcast.11, bf16[1,1,1792,1024]{3,2,1,0:T(8,128)(2,1)} %param.19), kind=kOutput, calls=%fused_computation.29 | convolution fusion | flops 2349465600 | bytes 7274496 | tf_op jit(solution)/shard_map/dot_general | solution.py:33
  101.3 4.3 %all-to-all-start.2 = ((bf16[16,40,1792]{2,1,0:T(8,128)(2,1)}), bf16[16,40,1792]{2,1,0:T(8,128)(2,1)}, u32[]{:S(2)}, u32[]{:S(2)}) async-start(bf16[16,40,1792]{2,1,0:T(8,128)(2,1)} %bitcast.24), calls=%async_computation.2 | async-start | bytes 4587520 | tf_op jit(solution)/shard_map/all_to_all | solution.py:25
  107.4 5.5 %fusion.32 = bf16[640,1024]{1,0:T(8,128)(2,1)S(1)} fusion(bf16[640,1792]{1,0:T(8,128)(2,1)} %bitcast.11, bf16[1,1,1792,1024]{3,2,1,0:T(8,128)(2,1)} %param.20), kind=kOutput, calls=%fused_computation.31 | convolution fusion | flops 2349465600 | bytes 7274496 | tf_op jit(solution)/shard_map/dot_general | solution.py:33
  120.4 28.6 %collective-permute-done.7 = bf16[320,1024]{1,0:T(8,128)(2,1)S(1)} collective-permute-done((bf16[320,1024]{1,0:T(8,128)(2,1)S(1)}, bf16[320,1024]{1,0:T(8,128)(2,1)S(1)}, u32[]{:S(2)}, u32[]{:S(2)}) %collective-permute-start.7) | collective-permute-done | bytes 655392 | tf_op jit(solution)/shard_map/ppermute | solution.py:16
  149.0 5.6 %fusion.35 = bf16[640,1024]{1,0:T(8,128)(2,1)S(1)} fusion(bf16[640,1792]{1,0:T(8,128)(2,1)} %bitcast.26, bf16[1,1,1024,1792]{3,2,1,0:T(8,128)(2,1)} %param.21), kind=kOutput, calls=%fused_computation.32 | convolution fusion | flops 2349465600 | bytes 7274496 | tf_op jit(solution)/shard_map/dot_general | solution.py:33
  163.2 4.9 %all-to-all-start.3 = ((bf16[16,40,1792]{2,1,0:T(8,128)(2,1)}), bf16[16,40,1792]{2,1,0:T(8,128)(2,1)S(1)}, u32[]{:S(2)}, u32[]{:S(2)}) async-start(bf16[16,40,1792]{2,1,0:T(8,128)(2,1)} %bitcast.111), calls=%async_computation.3 | async-start | bytes 4587520 | tf_op jit(solution)/shard_map/all_to_all | solution.py:25
  168.1 14.7 %collective-permute-done.10 = bf16[320,1024]{1,0:T(8,128)(2,1)} collective-permute-done((bf16[320,1024]{1,0:T(8,128)(2,1)S(1)}, bf16[320,1024]{1,0:T(8,128)(2,1)}, u32[]{:S(2)}, u32[]{:S(2)}) %collective-permute-start.10) | collective-permute-done | bytes 655392 | tf_op jit(solution)/shard_map/ppermute | solution.py:16
  187.4 9.5 %collective-permute-start.11 = (bf16[320,2176]{1,0:T(8,128)(2,1)}, bf16[320,2176]{1,0:T(8,128)(2,1)}, u32[]{:S(2)}, u32[]{:S(2)}) collective-permute-start(bf16[320,2176]{1,0:T(8,128)(2,1)} %pad_maximum_fusion), channel_id=1, source_target_pairs={{0,1},{1,0},{2,3},{3,2},{4,5},{5,4},{6,7},{7,6},{8,9},{9,8},{10,11... | collective-permute-start | bytes 4177928 | tf_op jit(solution)/shard_map/ppermute | solution.py:16
  196.9 8.8 %all-to-all-done.3.returned_ref = bf16[16,40,1792]{2,1,0:T(8,128)(2,1)S(1)} async-done(((bf16[16,40,1792]{2,1,0:T(8,128)(2,1)}), bf16[16,40,1792]{2,1,0:T(8,128)(2,1)S(1)}, u32[]{:S(2)}, u32[]{:S(2)}) %all-to-all-start.3) | async-done | bytes 2293792 | tf_op jit(solution)/shard_map/all_to_all | solution.py:25
  215.2 3.9 %all-to-all-start.4 = ((bf16[16,40,896]{2,1,0:T(8,128)(2,1)}), bf16[16,40,896]{2,1,0:T(8,128)(2,1)S(1)}, u32[]{:S(2)}, u32[]{:S(2)}) async-start(bf16[16,40,896]{2,1,0:T(8,128)(2,1)} %bitcast.110), calls=%async_computation.4 | async-start | bytes 2293760 | tf_op jit(solution)/shard_map/all_to_all | solution.py:25
  230.1 5.9 %all-to-all-done.4.returned_ref = bf16[16,40,896]{2,1,0:T(8,128)(2,1)S(1)} async-done(((bf16[16,40,896]{2,1,0:T(8,128)(2,1)}), bf16[16,40,896]{2,1,0:T(8,128)(2,1)S(1)}, u32[]{:S(2)}, u32[]{:S(2)}) %all-to-all-start.4) | async-done | bytes 1146912 | tf_op jit(solution)/shard_map/all_to_all | solution.py:25
  237.1 4.4 %all-to-all-start.5 = ((bf16[16,40,1024]{2,1,0:T(8,128)(2,1)}), bf16[16,40,1024]{2,1,0:T(8,128)(2,1)S(1)}, u32[]{:S(2)}, u32[]{:S(2)}) async-start(bf16[16,40,1024]{2,1,0:T(8,128)(2,1)} %bitcast.118), calls=%async_computation.5 | async-start | bytes 2621440 | tf_op jit(solution)/shard_map/all_to_all | solution.py:25
  246.8 5.9 %collective-permute-start.13 = (bf16[128,3072]{1,0:T(8,128)(2,1)}, bf16[128,3072]{1,0:T(8,128)(2,1)}, u32[]{:S(2)}, u32[]{:S(2)}) collective-permute-start(bf16[128,3072]{1,0:T(8,128)(2,1)} %get-tuple-element.29), channel_id=1, source_target_pairs={{0,112},{16,0},{32,16},{48,32},{64,48},{80,64},{96,80},{112,96},{1... | collective-permute-start | bytes 2359304 | tf_op jit(solution)/shard_map/ppermute | solution.py:21
  252.7 7.5 %all-to-all-done.5.returned_ref = bf16[16,40,1024]{2,1,0:T(8,128)(2,1)S(1)} async-done(((bf16[16,40,1024]{2,1,0:T(8,128)(2,1)}), bf16[16,40,1024]{2,1,0:T(8,128)(2,1)S(1)}, u32[]{:S(2)}, u32[]{:S(2)}) %all-to-all-start.5) | async-done | bytes 1310752 | tf_op jit(solution)/shard_map/all_to_all | solution.py:25
  264.2 6.0 %collective-permute-start.14 = (bf16[128,4096]{1,0:T(8,128)(2,1)}, bf16[128,4096]{1,0:T(8,128)(2,1)}, u32[]{:S(2)}, u32[]{:S(2)}) collective-permute-start(bf16[128,4096]{1,0:T(8,128)(2,1)} %shard_map.127), channel_id=1, source_target_pairs={{0,112},{16,0},{32,16},{48,32},{64,48},{80,64},{96,80},{112,96},{1... | collective-permute-start | bytes 3145736 | tf_op jit(solution)/shard_map/ppermute | solution.py:21
  274.1 27.9 %collective-permute-done.12.piece_ref = bf16[128,7168]{1,0:T(8,128)(2,1)} collective-permute-done((bf16[128,7168]{1,0:T(8,128)(2,1)}, bf16[128,7168]{1,0:T(8,128)(2,1)}, u32[]{:S(2)}, u32[]{:S(2)}) %collective-permute-start.12) | collective-permute-done | bytes 1835040 | tf_op jit(solution)/shard_map/ppermute | solution.py:21
  (116 shorter events, 70.7 us)
Async XLA Ops:
  5.7 37.0 %all-to-all-start = ((bf16[16,40,1792]{2,1,0:T(8,128)(2,1)}), bf16[16,40,1792]{2,1,0:T(8,128)(2,1)S(1)}, u32[]{:S(2)}, u32[]{:S(2)}) async-start(bf16[16,40,1792]{2,1,0:T(8,128)(2,1)} %bitcast.109), calls=%async_computation | async-start | bytes 4587520 | tf_op jit(solution)/shard_map/all_to_all | solution.py:25
  42.7 50.7 %all-to-all-start.1 = ((bf16[16,40,1792]{2,1,0:T(8,128)(2,1)}), bf16[16,40,1792]{2,1,0:T(8,128)(2,1)}, u32[]{:S(2)}, u32[]{:S(2)}) async-start(bf16[16,40,1792]{2,1,0:T(8,128)(2,1)} %bitcast.108), calls=%async_computation.1 | async-start | bytes 4587520 | tf_op jit(solution)/shard_map/all_to_all | solution.py:25
  54.6 3.4 %collective-permute-start = (bf16[320,1024]{1,0:T(8,128)(2,1)S(1)}, bf16[320,1024]{1,0:T(8,128)(2,1)S(1)}, u32[]{:S(2)}, u32[]{:S(2)}) collective-permute-start(bf16[320,1024]{1,0:T(8,128)(2,1)S(1)} %dynamic-slice_bitcast_fusion.4), channel_id=1, source_target_pairs={{0,1},{1,0},{2,3},{3,2},{4,5},{5,4},{6,7},{7,6},{8,9},{9,8},{10,11... | collective-permute-start | bytes 1966088 | tf_op jit(solution)/shard_map/ppermute | solution.py:16
  57.6 7.4 %collective-permute-start.3 = (bf16[320,1024]{1,0:T(8,128)(2,1)S(1)}, bf16[320,1024]{1,0:T(8,128)(2,1)S(1)}, u32[]{:S(2)}, u32[]{:S(2)}) collective-permute-start(bf16[320,1024]{1,0:T(8,128)(2,1)S(1)} %dynamic-slice_bitcast_fusion.2), channel_id=1, source_target_pairs={{0,1},{1,0},{2,3},{3,2},{4,5},{5,4},{6,7},{7,6},{8,9},{9,8},{10,11... | collective-permute-start | bytes 1966088 | tf_op jit(solution)/shard_map/ppermute | solution.py:16
  58.5 34.9 %collective-permute-start.1 = (bf16[320,1024]{1,0:T(8,128)(2,1)S(1)}, bf16[320,1024]{1,0:T(8,128)(2,1)}, u32[]{:S(2)}, u32[]{:S(2)}) collective-permute-start(bf16[320,1024]{1,0:T(8,128)(2,1)S(1)} %fusion.57), channel_id=1, source_target_pairs={{0,2},{1,3},{2,0},{3,1},{4,6},{5,7},{6,4},{7,5},{8,10},{9,11},{10,... | collective-permute-start | bytes 1966088 | tf_op jit(solution)/shard_map/ppermute | solution.py:16
  65.2 42.2 %collective-permute-start.4 = (bf16[320,1024]{1,0:T(8,128)(2,1)S(1)}, bf16[320,1024]{1,0:T(8,128)(2,1)S(1)}, u32[]{:S(2)}, u32[]{:S(2)}) collective-permute-start(bf16[320,1024]{1,0:T(8,128)(2,1)S(1)} %fusion.55), channel_id=1, source_target_pairs={{0,2},{1,3},{2,0},{3,1},{4,6},{5,7},{6,4},{7,5},{8,10},{9,11},{10,... | collective-permute-start | bytes 1966088 | tf_op jit(solution)/shard_map/ppermute | solution.py:16
  99.8 14.3 %collective-permute-start.2 = (bf16[320,1024]{1,0:T(8,128)(2,1)S(1)}, bf16[320,1024]{1,0:T(8,128)(2,1)S(1)}, u32[]{:S(2)}, u32[]{:S(2)}) collective-permute-start(bf16[320,1024]{1,0:T(8,128)(2,1)S(1)} %dynamic-slice_bitcast_fusion.3), channel_id=1, source_target_pairs={{0,1},{1,0},{2,3},{3,2},{4,5},{5,4},{6,7},{7,6},{8,9},{9,8},{10,11... | collective-permute-start | bytes 1966088 | tf_op jit(solution)/shard_map/ppermute | solution.py:16
  101.3 47.7 %all-to-all-start.2 = ((bf16[16,40,1792]{2,1,0:T(8,128)(2,1)}), bf16[16,40,1792]{2,1,0:T(8,128)(2,1)}, u32[]{:S(2)}, u32[]{:S(2)}) async-start(bf16[16,40,1792]{2,1,0:T(8,128)(2,1)} %bitcast.24), calls=%async_computation.2 | async-start | bytes 4587520 | tf_op jit(solution)/shard_map/all_to_all | solution.py:25
  113.0 2.9 collective-permute-start.5
  118.0 2.4 collective-permute-start.6
  118.7 30.3 %collective-permute-start.7 = (bf16[320,1024]{1,0:T(8,128)(2,1)S(1)}, bf16[320,1024]{1,0:T(8,128)(2,1)S(1)}, u32[]{:S(2)}, u32[]{:S(2)}) collective-permute-start(bf16[320,1024]{1,0:T(8,128)(2,1)S(1)} %fusion.56), channel_id=1, source_target_pairs={{0,2},{1,3},{2,0},{3,1},{4,6},{5,7},{6,4},{7,5},{8,10},{9,11},{10,... | collective-permute-start | bytes 1966088 | tf_op jit(solution)/shard_map/ppermute | solution.py:16
  118.7 44.4 %collective-permute-start.9 = (bf16[320,1024]{1,0:T(8,128)(2,1)S(1)}, bf16[320,1024]{1,0:T(8,128)(2,1)}, u32[]{:S(2)}, u32[]{:S(2)}) collective-permute-start(bf16[320,1024]{1,0:T(8,128)(2,1)S(1)} %fusion.54), channel_id=1, source_target_pairs={{0,2},{1,3},{2,0},{3,1},{4,6},{5,7},{6,4},{7,5},{8,10},{9,11},{10,... | collective-permute-start | bytes 1966088 | tf_op jit(solution)/shard_map/ppermute | solution.py:16
  120.4 34.2 %copy-start.25 = (bf16[320,1024]{1,0:T(8,128)(2,1)}, bf16[320,1024]{1,0:T(8,128)(2,1)S(1)}, u32[]{:S(2)}) copy-start(bf16[320,1024]{1,0:T(8,128)(2,1)S(1)} %collective-permute-done.6) | copy-start | bytes 1966084
  154.7 5.5 %collective-permute-start.8 = (bf16[320,1024]{1,0:T(8,128)(2,1)S(1)}, bf16[320,1024]{1,0:T(8,128)(2,1)S(1)}, u32[]{:S(2)}, u32[]{:S(2)}) collective-permute-start(bf16[320,1024]{1,0:T(8,128)(2,1)S(1)} %dynamic-slice_bitcast_fusion), channel_id=1, source_target_pairs={{0,1},{1,0},{2,3},{3,2},{4,5},{5,4},{6,7},{7,6},{8,9},{9,8},{10,11... | collective-permute-start | bytes 1966088 | tf_op jit(solution)/shard_map/ppermute | solution.py:16
  163.1 19.6 %collective-permute-start.10 = (bf16[320,1024]{1,0:T(8,128)(2,1)S(1)}, bf16[320,1024]{1,0:T(8,128)(2,1)}, u32[]{:S(2)}, u32[]{:S(2)}) collective-permute-start(bf16[320,1024]{1,0:T(8,128)(2,1)S(1)} %fusion.53), channel_id=1, source_target_pairs={{0,2},{1,3},{2,0},{3,1},{4,6},{5,7},{6,4},{7,5},{8,10},{9,11},{10,... | collective-permute-start | bytes 1966088 | tf_op jit(solution)/shard_map/ppermute | solution.py:16
  163.2 42.6 %all-to-all-start.3 = ((bf16[16,40,1792]{2,1,0:T(8,128)(2,1)}), bf16[16,40,1792]{2,1,0:T(8,128)(2,1)S(1)}, u32[]{:S(2)}, u32[]{:S(2)}) async-start(bf16[16,40,1792]{2,1,0:T(8,128)(2,1)} %bitcast.111), calls=%async_computation.3 | async-start | bytes 4587520 | tf_op jit(solution)/shard_map/all_to_all | solution.py:25
  187.4 18.3 %collective-permute-start.11 = (bf16[320,2176]{1,0:T(8,128)(2,1)}, bf16[320,2176]{1,0:T(8,128)(2,1)}, u32[]{:S(2)}, u32[]{:S(2)}) collective-permute-start(bf16[320,2176]{1,0:T(8,128)(2,1)} %pad_maximum_fusion), channel_id=1, source_target_pairs={{0,1},{1,0},{2,3},{3,2},{4,5},{5,4},{6,7},{7,6},{8,9},{9,8},{10,11... | collective-permute-start | bytes 4177928 | tf_op jit(solution)/shard_map/ppermute | solution.py:16
  215.2 20.8 %all-to-all-start.4 = ((bf16[16,40,896]{2,1,0:T(8,128)(2,1)}), bf16[16,40,896]{2,1,0:T(8,128)(2,1)S(1)}, u32[]{:S(2)}, u32[]{:S(2)}) async-start(bf16[16,40,896]{2,1,0:T(8,128)(2,1)} %bitcast.110), calls=%async_computation.4 | async-start | bytes 2293760 | tf_op jit(solution)/shard_map/all_to_all | solution.py:25
  230.1 11.4 %copy-start.6 = (bf16[1,7168]{1,0:T(2,128)(2,1)S(1)}, bf16[1,7168]{1,0:T(2,128)(2,1)}, u32[]{:S(2)}) copy-start(bf16[1,7168]{1,0:T(2,128)(2,1)} %norm_ref.7) | copy-start | bytes 43012
  230.1 11.4 %copy-start.7 = (s32[1,128,1]{1,2,0:T(1,128)S(1)}, s32[1,128,1]{1,2,0:T(1,128)}, u32[]{:S(2)}) copy-start(s32[1,128,1]{1,2,0:T(1,128)} %param.16) | copy-start | bytes 1540
  237.1 23.1 %all-to-all-start.5 = ((bf16[16,40,1024]{2,1,0:T(8,128)(2,1)}), bf16[16,40,1024]{2,1,0:T(8,128)(2,1)S(1)}, u32[]{:S(2)}, u32[]{:S(2)}) async-start(bf16[16,40,1024]{2,1,0:T(8,128)(2,1)} %bitcast.118), calls=%async_computation.5 | async-start | bytes 2621440 | tf_op jit(solution)/shard_map/all_to_all | solution.py:25
  246.8 26.2 %collective-permute-start.13 = (bf16[128,3072]{1,0:T(8,128)(2,1)}, bf16[128,3072]{1,0:T(8,128)(2,1)}, u32[]{:S(2)}, u32[]{:S(2)}) collective-permute-start(bf16[128,3072]{1,0:T(8,128)(2,1)} %get-tuple-element.29), channel_id=1, source_target_pairs={{0,112},{16,0},{32,16},{48,32},{64,48},{80,64},{96,80},{112,96},{1... | collective-permute-start | bytes 2359304 | tf_op jit(solution)/shard_map/ppermute | solution.py:21
  252.7 49.4 %collective-permute-start.12 = (bf16[128,7168]{1,0:T(8,128)(2,1)}, bf16[128,7168]{1,0:T(8,128)(2,1)}, u32[]{:S(2)}, u32[]{:S(2)}) collective-permute-start(bf16[128,7168]{1,0:T(8,128)(2,1)} %shard_map.125), channel_id=1, source_target_pairs={{0,16},{16,32},{32,48},{48,64},{64,80},{80,96},{96,112},{112,0},{1... | collective-permute-start | bytes 5505032 | tf_op jit(solution)/shard_map/ppermute | solution.py:21
  264.2 40.7 %collective-permute-start.14 = (bf16[128,4096]{1,0:T(8,128)(2,1)}, bf16[128,4096]{1,0:T(8,128)(2,1)}, u32[]{:S(2)}, u32[]{:S(2)}) collective-permute-start(bf16[128,4096]{1,0:T(8,128)(2,1)} %shard_map.127), channel_id=1, source_target_pairs={{0,112},{16,0},{32,16},{48,32},{64,48},{80,64},{96,80},{112,96},{1... | collective-permute-start | bytes 3145736 | tf_op jit(solution)/shard_map/ppermute | solution.py:21
  (27 other events, 94.7 us)

commit v2 on v1

--- a/solution.py
+++ b/solution.py
@@ -381,13 +381,13 @@
         factors,
         second_back,
     )
-    arrived_input = local_call(copy_kernel, whole, after(arrived_input, second_out))
     first_out = passed_along(first_out, "pp", -1)
     first_out = local_call(
         copy_kernel, jax.ShapeDtypeStruct(first_out.shape, jnp.bfloat16), first_out, flops=1 << 40
     )
     second_out = passed_along(second_out, "pp", -1)
     arrived_grad = local_call(joined_kernel, whole, first_out, second_out)
+    arrived_input = local_call(copy_kernel, whole, after(arrived_input, arrived_grad))
     return (arrived_input[None], arrived_grad[None])
 
 

time: 309 us -> 306 us (level)
  transfers between devices with their start and end apart: 21 -> 21, of which waited for: 13 -> 14; matrix products, arithmetic and copies ran while one was open for 14% -> 14% of each run, Pallas kernels for 7% -> 7%
where the time goes in v2:
time: 306 us; the launch traced here: 305 us
  waiting for transfers between devices  153 us (50%)
  starting transfers between devices  61.6 us (20%)
  matrix products  39.8 us (13%)
  Pallas kernels  30 us (10%)
  other arithmetic  10.9 us (4%)
  local copies, waits for them, and re-layouts  8.61 us (3%)
    ppermute x12, waiting for transfers between devices, from_partner(): lax.ppermute(value, axis, [(i, i ^ 1 << bit) for i in range(lax.axis_size...  77.5 us
    all_to_all x6, waiting for transfers between devices, exchange(): return lax.all_to_all(value, 'ep', split_axis=0, concat_axis=0, tiled=True)  47.4 us
    dot_general x10, matrix products, contract(): lax.dot_general(left, right, (((left_dim,), (right_dim,)), ((), ())), pre...  39.8 us
    all_to_all x6, starting transfers between devices, exchange(): return lax.all_to_all(value, 'ep', split_axis=0, concat_axis=0, tiled=True)  31.6 us
    ppermute x3, waiting for transfers between devices, passed_along(): lax.ppermute(value, axis, [(i, (i + by) % count) for i in range(count)])  28.1 us
    ppermute x12, starting transfers between devices, from_partner(): lax.ppermute(value, axis, [(i, i ^ 1 << bit) for i in range(lax.axis_size...  18 us
    pallas_call x3, Pallas kernels, to_experts(): pl.pallas_call(kernel, out_shape=jax.ShapeDtypeStruct((experts, 4, capaci...  15 us
    pallas_call x6, Pallas kernels, local_call(): pl.pallas_call(kernel, out_shape=shapes, in_specs=[whole] * len(arrays),...  15 us
  transfers between devices with their start and end apart: 21, of which 14 were waited for; matrix products, arithmetic and copies ran while one was open for 14% of the time, Pallas kernels for 7%

profile of v2, /device:TPU:1, one launch (start us, length us, event | category | flops | bytes accessed | tf_op | source)
XLA Modules:
  0.0 304.9 jit_solution(7259627456553093040)
XLA Ops:
  0.6 5.1 %shard_map.122 = bf16[4,4,40,1792]{3,2,1,0:T(8,128)(2,1)} custom-call(s32[1,128]{1,0:T(1,128)} %bitcast.106, bf16[128,7168]{1,0:T(8,128)(2,1)} %bitcast.100, bf16[1,7168]{1,0:T(2,128)(2,1)} %norm_ref.7), custom_call_target="tpu_custom_call" | custom-call | flops 536870912 | bytes 8388608 | tf_op jit(solution)/shard_map/pallas_call | solution.py:104
  5.7 6.9 %all-to-all-start = ((bf16[16,40,1792]{2,1,0:T(8,128)(2,1)}), bf16[16,40,1792]{2,1,0:T(8,128)(2,1)S(1)}, u32[]{:S(2)}, u32[]{:S(2)}) async-start(bf16[16,40,1792]{2,1,0:T(8,128)(2,1)} %bitcast.109), calls=%async_computation | async-start | bytes 4587520 | tf_op jit(solution)/shard_map/all_to_all | solution.py:25
  12.6 5.1 %shard_map.123 = bf16[4,4,40,1792]{3,2,1,0:T(8,128)(2,1)} custom-call(s32[1,128]{1,0:T(1,128)} %bitcast.102, bf16[128,7168]{1,0:T(8,128)(2,1)} %bitcast.94, bf16[1,7168]{1,0:T(2,128)(2,1)} %norm_ref.7), custom_call_target="tpu_custom_call" | custom-call | flops 536870912 | bytes 8388608 | tf_op jit(solution)/shard_map/pallas_call | solution.py:104
  17.7 25.0 %all-to-all-done = bf16[16,40,1792]{2,1,0:T(8,128)(2,1)S(1)} async-done(((bf16[16,40,1792]{2,1,0:T(8,128)(2,1)}), bf16[16,40,1792]{2,1,0:T(8,128)(2,1)S(1)}, u32[]{:S(2)}, u32[]{:S(2)}) %all-to-all-start) | async-done | bytes 2293792 | tf_op jit(solution)/shard_map/all_to_all | solution.py:25
  42.7 7.1 %all-to-all-start.1 = ((bf16[16,40,1792]{2,1,0:T(8,128)(2,1)}), bf16[16,40,1792]{2,1,0:T(8,128)(2,1)}, u32[]{:S(2)}, u32[]{:S(2)}) async-start(bf16[16,40,1792]{2,1,0:T(8,128)(2,1)} %bitcast.108), calls=%async_computation.1 | async-start | bytes 4587520 | tf_op jit(solution)/shard_map/all_to_all | solution.py:25
  49.9 4.7 %fusion.23 = bf16[640,1024]{1,0:T(8,128)(2,1)S(1)} fusion(bf16[640,1792]{1,0:T(8,128)(2,1)S(1)} %bitcast.112, bf16[1,1,1792,1024]{3,2,1,0:T(8,128)(2,1)} %param.19), kind=kOutput, calls=%fused_computation.28 | convolution fusion | flops 2349465600 | bytes 7274496 | tf_op jit(solution)/shard_map/dot_general | solution.py:33
  60.1 4.8 %shard_map.124 = bf16[4,4,40,1792]{3,2,1,0:T(8,128)(2,1)} custom-call(s32[1,128]{1,0:T(1,128)} %bitcast.103, f32[1,128]{1,0:T(1,128)} %weight_ref.2, bf16[128,7168]{1,0:T(8,128)(2,1)} %bitcast.97), custom_call_target="tpu_custom_call" | custom-call | flops 536870912 | bytes 8388608 | tf_op jit(solution)/shard_map/pallas_call | solution.py:104
  65.3 28.1 %collective-permute-done.1 = bf16[320,1024]{1,0:T(8,128)(2,1)} collective-permute-done((bf16[320,1024]{1,0:T(8,128)(2,1)S(1)}, bf16[320,1024]{1,0:T(8,128)(2,1)}, u32[]{:S(2)}, u32[]{:S(2)}) %collective-permute-start.1) | collective-permute-done | bytes 655392 | tf_op jit(solution)/shard_map/ppermute | solution.py:16
  93.5 5.3 %fusion.26 = bf16[640,1024]{1,0:T(8,128)(2,1)S(1)} fusion(bf16[640,1792]{1,0:T(8,128)(2,1)} %bitcast.11, bf16[1,1,1792,1024]{3,2,1,0:T(8,128)(2,1)} %param.19), kind=kOutput, calls=%fused_computation.29 | convolution fusion | flops 2349465600 | bytes 7274496 | tf_op jit(solution)/shard_map/dot_general | solution.py:33
  101.3 4.3 %all-to-all-start.2 = ((bf16[16,40,1792]{2,1,0:T(8,128)(2,1)}), bf16[16,40,1792]{2,1,0:T(8,128)(2,1)}, u32[]{:S(2)}, u32[]{:S(2)}) async-start(bf16[16,40,1792]{2,1,0:T(8,128)(2,1)} %bitcast.24), calls=%async_computation.2 | async-start | bytes 4587520 | tf_op jit(solution)/shard_map/all_to_all | solution.py:25
  107.4 5.5 %fusion.32 = bf16[640,1024]{1,0:T(8,128)(2,1)S(1)} fusion(bf16[640,1792]{1,0:T(8,128)(2,1)} %bitcast.11, bf16[1,1,1792,1024]{3,2,1,0:T(8,128)(2,1)} %param.20), kind=kOutput, calls=%fused_computation.31 | convolution fusion | flops 2349465600 | bytes 7274496 | tf_op jit(solution)/shard_map/dot_general | solution.py:33
  120.4 28.6 %collective-permute-done.7 = bf16[320,1024]{1,0:T(8,128)(2,1)S(1)} collective-permute-done((bf16[320,1024]{1,0:T(8,128)(2,1)S(1)}, bf16[320,1024]{1,0:T(8,128)(2,1)S(1)}, u32[]{:S(2)}, u32[]{:S(2)}) %collective-permute-start.7) | collective-permute-done | bytes 655392 | tf_op jit(solution)/shard_map/ppermute | solution.py:16
  149.0 5.6 %fusion.35 = bf16[640,1024]{1,0:T(8,128)(2,1)S(1)} fusion(bf16[640,1792]{1,0:T(8,128)(2,1)} %bitcast.26, bf16[1,1,1024,1792]{3,2,1,0:T(8,128)(2,1)} %param.21), kind=kOutput, calls=%fused_computation.32 | convolution fusion | flops 2349465600 | bytes 7274496 | tf_op jit(solution)/shard_map/dot_general | solution.py:33
  163.2 4.9 %all-to-all-start.3 = ((bf16[16,40,1792]{2,1,0:T(8,128)(2,1)}), bf16[16,40,1792]{2,1,0:T(8,128)(2,1)S(1)}, u32[]{:S(2)}, u32[]{:S(2)}) async-start(bf16[16,40,1792]{2,1,0:T(8,128)(2,1)} %bitcast.111), calls=%async_computation.3 | async-start | bytes 4587520 | tf_op jit(solution)/shard_map/all_to_all | solution.py:25
  168.1 14.7 %collective-permute-done.10 = bf16[320,1024]{1,0:T(8,128)(2,1)} collective-permute-done((bf16[320,1024]{1,0:T(8,128)(2,1)S(1)}, bf16[320,1024]{1,0:T(8,128)(2,1)}, u32[]{:S(2)}, u32[]{:S(2)}) %collective-permute-start.10) | collective-permute-done | bytes 655392 | tf_op jit(solution)/shard_map/ppermute | solution.py:16
  187.4 9.5 %collective-permute-start.11 = (bf16[320,2176]{1,0:T(8,128)(2,1)}, bf16[320,2176]{1,0:T(8,128)(2,1)}, u32[]{:S(2)}, u32[]{:S(2)}) collective-permute-start(bf16[320,2176]{1,0:T(8,128)(2,1)} %pad_maximum_fusion), channel_id=1, source_target_pairs={{0,1},{1,0},{2,3},{3,2},{4,5},{5,4},{6,7},{7,6},{8,9},{9,8},{10,11... | collective-permute-start | bytes 4177928 | tf_op jit(solution)/shard_map/ppermute | solution.py:16
  196.9 8.8 %all-to-all-done.3.returned_ref = bf16[16,40,1792]{2,1,0:T(8,128)(2,1)S(1)} async-done(((bf16[16,40,1792]{2,1,0:T(8,128)(2,1)}), bf16[16,40,1792]{2,1,0:T(8,128)(2,1)S(1)}, u32[]{:S(2)}, u32[]{:S(2)}) %all-to-all-start.3) | async-done | bytes 2293792 | tf_op jit(solution)/shard_map/all_to_all | solution.py:25
  230.1 5.9 %all-to-all-done.4.returned_ref = bf16[16,40,896]{2,1,0:T(8,128)(2,1)S(1)} async-done(((bf16[16,40,896]{2,1,0:T(8,128)(2,1)}), bf16[16,40,896]{2,1,0:T(8,128)(2,1)S(1)}, u32[]{:S(2)}, u32[]{:S(2)}) %all-to-all-start.4) | async-done | bytes 1146912 | tf_op jit(solution)/shard_map/all_to_all | solution.py:25
  237.1 4.4 %all-to-all-start.5 = ((bf16[16,40,1024]{2,1,0:T(8,128)(2,1)}), bf16[16,40,1024]{2,1,0:T(8,128)(2,1)S(1)}, u32[]{:S(2)}, u32[]{:S(2)}) async-start(bf16[16,40,1024]{2,1,0:T(8,128)(2,1)} %bitcast.118), calls=%async_computation.5 | async-start | bytes 2621440 | tf_op jit(solution)/shard_map/all_to_all | solution.py:25
  246.7 5.9 %collective-permute-start.13 = (bf16[128,3072]{1,0:T(8,128)(2,1)}, bf16[128,3072]{1,0:T(8,128)(2,1)}, u32[]{:S(2)}, u32[]{:S(2)}) collective-permute-start(bf16[128,3072]{1,0:T(8,128)(2,1)} %get-tuple-element.26), channel_id=1, source_target_pairs={{0,112},{16,0},{32,16},{48,32},{64,48},{80,64},{96,80},{112,96},{1... | collective-permute-start | bytes 2359304 | tf_op jit(solution)/shard_map/ppermute | solution.py:21
  252.6 7.6 %all-to-all-done.5.returned_ref = bf16[16,40,1024]{2,1,0:T(8,128)(2,1)S(1)} async-done(((bf16[16,40,1024]{2,1,0:T(8,128)(2,1)}), bf16[16,40,1024]{2,1,0:T(8,128)(2,1)S(1)}, u32[]{:S(2)}, u32[]{:S(2)}) %all-to-all-start.5) | async-done | bytes 1310752 | tf_op jit(solution)/shard_map/all_to_all | solution.py:25
  264.2 6.0 %collective-permute-start.14 = (bf16[128,4096]{1,0:T(8,128)(2,1)}, bf16[128,4096]{1,0:T(8,128)(2,1)}, u32[]{:S(2)}, u32[]{:S(2)}) collective-permute-start(bf16[128,4096]{1,0:T(8,128)(2,1)} %shard_map.128), channel_id=1, source_target_pairs={{0,112},{16,0},{32,16},{48,32},{64,48},{80,64},{96,80},{112,96},{1... | collective-permute-start | bytes 3145736 | tf_op jit(solution)/shard_map/ppermute | solution.py:21
  274.1 21.3 %collective-permute-done.14.second_ref = bf16[128,4096]{1,0:T(8,128)(2,1)} collective-permute-done((bf16[128,4096]{1,0:T(8,128)(2,1)}, bf16[128,4096]{1,0:T(8,128)(2,1)}, u32[]{:S(2)}, u32[]{:S(2)}) %collective-permute-start.14) | collective-permute-done | bytes 1048608 | tf_op jit(solution)/shard_map/ppermute | solution.py:21
  298.0 4.1 %collective-permute-done.12.piece_ref = bf16[128,7168]{1,0:T(8,128)(2,1)} collective-permute-done((bf16[128,7168]{1,0:T(8,128)(2,1)}, bf16[128,7168]{1,0:T(8,128)(2,1)}, u32[]{:S(2)}, u32[]{:S(2)}) %collective-permute-start.12) | collective-permute-done | bytes 1835040 | tf_op jit(solution)/shard_map/ppermute | solution.py:21
  (116 shorter events, 74.5 us)
Async XLA Ops:
  5.7 37.0 %all-to-all-start = ((bf16[16,40,1792]{2,1,0:T(8,128)(2,1)}), bf16[16,40,1792]{2,1,0:T(8,128)(2,1)S(1)}, u32[]{:S(2)}, u32[]{:S(2)}) async-start(bf16[16,40,1792]{2,1,0:T(8,128)(2,1)} %bitcast.109), calls=%async_computation | async-start | bytes 4587520 | tf_op jit(solution)/shard_map/all_to_all | solution.py:25
  42.7 50.7 %all-to-all-start.1 = ((bf16[16,40,1792]{2,1,0:T(8,128)(2,1)}), bf16[16,40,1792]{2,1,0:T(8,128)(2,1)}, u32[]{:S(2)}, u32[]{:S(2)}) async-start(bf16[16,40,1792]{2,1,0:T(8,128)(2,1)} %bitcast.108), calls=%async_computation.1 | async-start | bytes 4587520 | tf_op jit(solution)/shard_map/all_to_all | solution.py:25
  54.6 3.4 %collective-permute-start = (bf16[320,1024]{1,0:T(8,128)(2,1)S(1)}, bf16[320,1024]{1,0:T(8,128)(2,1)S(1)}, u32[]{:S(2)}, u32[]{:S(2)}) collective-permute-start(bf16[320,1024]{1,0:T(8,128)(2,1)S(1)} %dynamic-slice_bitcast_fusion.4), channel_id=1, source_target_pairs={{0,1},{1,0},{2,3},{3,2},{4,5},{5,4},{6,7},{7,6},{8,9},{9,8},{10,11... | collective-permute-start | bytes 1966088 | tf_op jit(solution)/shard_map/ppermute | solution.py:16
  57.6 7.4 %collective-permute-start.3 = (bf16[320,1024]{1,0:T(8,128)(2,1)S(1)}, bf16[320,1024]{1,0:T(8,128)(2,1)S(1)}, u32[]{:S(2)}, u32[]{:S(2)}) collective-permute-start(bf16[320,1024]{1,0:T(8,128)(2,1)S(1)} %dynamic-slice_bitcast_fusion.2), channel_id=1, source_target_pairs={{0,1},{1,0},{2,3},{3,2},{4,5},{5,4},{6,7},{7,6},{8,9},{9,8},{10,11... | collective-permute-start | bytes 1966088 | tf_op jit(solution)/shard_map/ppermute | solution.py:16
  58.5 34.9 %collective-permute-start.1 = (bf16[320,1024]{1,0:T(8,128)(2,1)S(1)}, bf16[320,1024]{1,0:T(8,128)(2,1)}, u32[]{:S(2)}, u32[]{:S(2)}) collective-permute-start(bf16[320,1024]{1,0:T(8,128)(2,1)S(1)} %fusion.57), channel_id=1, source_target_pairs={{0,2},{1,3},{2,0},{3,1},{4,6},{5,7},{6,4},{7,5},{8,10},{9,11},{10,... | collective-permute-start | bytes 1966088 | tf_op jit(solution)/shard_map/ppermute | solution.py:16
  65.2 42.2 %collective-permute-start.4 = (bf16[320,1024]{1,0:T(8,128)(2,1)S(1)}, bf16[320,1024]{1,0:T(8,128)(2,1)S(1)}, u32[]{:S(2)}, u32[]{:S(2)}) collective-permute-start(bf16[320,1024]{1,0:T(8,128)(2,1)S(1)} %fusion.55), channel_id=1, source_target_pairs={{0,2},{1,3},{2,0},{3,1},{4,6},{5,7},{6,4},{7,5},{8,10},{9,11},{10,... | collective-permute-start | bytes 1966088 | tf_op jit(solution)/shard_map/ppermute | solution.py:16
  99.8 14.3 %collective-permute-start.2 = (bf16[320,1024]{1,0:T(8,128)(2,1)S(1)}, bf16[320,1024]{1,0:T(8,128)(2,1)S(1)}, u32[]{:S(2)}, u32[]{:S(2)}) collective-permute-start(bf16[320,1024]{1,0:T(8,128)(2,1)S(1)} %dynamic-slice_bitcast_fusion.3), channel_id=1, source_target_pairs={{0,1},{1,0},{2,3},{3,2},{4,5},{5,4},{6,7},{7,6},{8,9},{9,8},{10,11... | collective-permute-start | bytes 1966088 | tf_op jit(solution)/shard_map/ppermute | solution.py:16
  101.3 47.7 %all-to-all-start.2 = ((bf16[16,40,1792]{2,1,0:T(8,128)(2,1)}), bf16[16,40,1792]{2,1,0:T(8,128)(2,1)}, u32[]{:S(2)}, u32[]{:S(2)}) async-start(bf16[16,40,1792]{2,1,0:T(8,128)(2,1)} %bitcast.24), calls=%async_computation.2 | async-start | bytes 4587520 | tf_op jit(solution)/shard_map/all_to_all | solution.py:25
  113.0 2.9 collective-permute-start.5
  118.0 2.4 collective-permute-start.6
  118.7 30.3 %collective-permute-start.7 = (bf16[320,1024]{1,0:T(8,128)(2,1)S(1)}, bf16[320,1024]{1,0:T(8,128)(2,1)S(1)}, u32[]{:S(2)}, u32[]{:S(2)}) collective-permute-start(bf16[320,1024]{1,0:T(8,128)(2,1)S(1)} %fusion.56), channel_id=1, source_target_pairs={{0,2},{1,3},{2,0},{3,1},{4,6},{5,7},{6,4},{7,5},{8,10},{9,11},{10,... | collective-permute-start | bytes 1966088 | tf_op jit(solution)/shard_map/ppermute | solution.py:16
  118.7 44.4 %collective-permute-start.9 = (bf16[320,1024]{1,0:T(8,128)(2,1)S(1)}, bf16[320,1024]{1,0:T(8,128)(2,1)}, u32[]{:S(2)}, u32[]{:S(2)}) collective-permute-start(bf16[320,1024]{1,0:T(8,128)(2,1)S(1)} %fusion.54), channel_id=1, source_target_pairs={{0,2},{1,3},{2,0},{3,1},{4,6},{5,7},{6,4},{7,5},{8,10},{9,11},{10,... | collective-permute-start | bytes 1966088 | tf_op jit(solution)/shard_map/ppermute | solution.py:16
  120.4 34.2 %copy-start.25 = (bf16[320,1024]{1,0:T(8,128)(2,1)}, bf16[320,1024]{1,0:T(8,128)(2,1)S(1)}, u32[]{:S(2)}) copy-start(bf16[320,1024]{1,0:T(8,128)(2,1)S(1)} %collective-permute-done.6) | copy-start | bytes 1966084
  154.7 5.5 %collective-permute-start.8 = (bf16[320,1024]{1,0:T(8,128)(2,1)S(1)}, bf16[320,1024]{1,0:T(8,128)(2,1)S(1)}, u32[]{:S(2)}, u32[]{:S(2)}) collective-permute-start(bf16[320,1024]{1,0:T(8,128)(2,1)S(1)} %dynamic-slice_bitcast_fusion), channel_id=1, source_target_pairs={{0,1},{1,0},{2,3},{3,2},{4,5},{5,4},{6,7},{7,6},{8,9},{9,8},{10,11... | collective-permute-start | bytes 1966088 | tf_op jit(solution)/shard_map/ppermute | solution.py:16
  163.1 19.6 %collective-permute-start.10 = (bf16[320,1024]{1,0:T(8,128)(2,1)S(1)}, bf16[320,1024]{1,0:T(8,128)(2,1)}, u32[]{:S(2)}, u32[]{:S(2)}) collective-permute-start(bf16[320,1024]{1,0:T(8,128)(2,1)S(1)} %fusion.53), channel_id=1, source_target_pairs={{0,2},{1,3},{2,0},{3,1},{4,6},{5,7},{6,4},{7,5},{8,10},{9,11},{10,... | collective-permute-start | bytes 1966088 | tf_op jit(solution)/shard_map/ppermute | solution.py:16
  163.2 42.6 %all-to-all-start.3 = ((bf16[16,40,1792]{2,1,0:T(8,128)(2,1)}), bf16[16,40,1792]{2,1,0:T(8,128)(2,1)S(1)}, u32[]{:S(2)}, u32[]{:S(2)}) async-start(bf16[16,40,1792]{2,1,0:T(8,128)(2,1)} %bitcast.111), calls=%async_computation.3 | async-start | bytes 4587520 | tf_op jit(solution)/shard_map/all_to_all | solution.py:25
  187.4 18.3 %collective-permute-start.11 = (bf16[320,2176]{1,0:T(8,128)(2,1)}, bf16[320,2176]{1,0:T(8,128)(2,1)}, u32[]{:S(2)}, u32[]{:S(2)}) collective-permute-start(bf16[320,2176]{1,0:T(8,128)(2,1)} %pad_maximum_fusion), channel_id=1, source_target_pairs={{0,1},{1,0},{2,3},{3,2},{4,5},{5,4},{6,7},{7,6},{8,9},{9,8},{10,11... | collective-permute-start | bytes 4177928 | tf_op jit(solution)/shard_map/ppermute | solution.py:16
  215.2 20.8 %all-to-all-start.4 = ((bf16[16,40,896]{2,1,0:T(8,128)(2,1)}), bf16[16,40,896]{2,1,0:T(8,128)(2,1)S(1)}, u32[]{:S(2)}, u32[]{:S(2)}) async-start(bf16[16,40,896]{2,1,0:T(8,128)(2,1)} %bitcast.110), calls=%async_computation.4 | async-start | bytes 2293760 | tf_op jit(solution)/shard_map/all_to_all | solution.py:25
  230.1 11.4 %copy-start.6 = (bf16[1,7168]{1,0:T(2,128)(2,1)S(1)}, bf16[1,7168]{1,0:T(2,128)(2,1)}, u32[]{:S(2)}) copy-start(bf16[1,7168]{1,0:T(2,128)(2,1)} %norm_ref.7) | copy-start | bytes 43012
  230.1 11.4 %copy-start.7 = (s32[1,128,1]{1,2,0:T(1,128)S(1)}, s32[1,128,1]{1,2,0:T(1,128)}, u32[]{:S(2)}) copy-start(s32[1,128,1]{1,2,0:T(1,128)} %param.16) | copy-start | bytes 1540
  237.1 23.1 %all-to-all-start.5 = ((bf16[16,40,1024]{2,1,0:T(8,128)(2,1)}), bf16[16,40,1024]{2,1,0:T(8,128)(2,1)S(1)}, u32[]{:S(2)}, u32[]{:S(2)}) async-start(bf16[16,40,1024]{2,1,0:T(8,128)(2,1)} %bitcast.118), calls=%async_computation.5 | async-start | bytes 2621440 | tf_op jit(solution)/shard_map/all_to_all | solution.py:25
  246.7 26.3 %collective-permute-start.13 = (bf16[128,3072]{1,0:T(8,128)(2,1)}, bf16[128,3072]{1,0:T(8,128)(2,1)}, u32[]{:S(2)}, u32[]{:S(2)}) collective-permute-start(bf16[128,3072]{1,0:T(8,128)(2,1)} %get-tuple-element.26), channel_id=1, source_target_pairs={{0,112},{16,0},{32,16},{48,32},{64,48},{80,64},{96,80},{112,96},{1... | collective-permute-start | bytes 2359304 | tf_op jit(solution)/shard_map/ppermute | solution.py:21
  252.6 49.5 %collective-permute-start.12 = (bf16[128,7168]{1,0:T(8,128)(2,1)}, bf16[128,7168]{1,0:T(8,128)(2,1)}, u32[]{:S(2)}, u32[]{:S(2)}) collective-permute-start(bf16[128,7168]{1,0:T(8,128)(2,1)} %shard_map.125), channel_id=1, source_target_pairs={{0,16},{16,32},{32,48},{48,64},{64,80},{80,96},{96,112},{112,0},{1... | collective-permute-start | bytes 5505032 | tf_op jit(solution)/shard_map/ppermute | solution.py:21
  264.2 31.2 %collective-permute-start.14 = (bf16[128,4096]{1,0:T(8,128)(2,1)}, bf16[128,4096]{1,0:T(8,128)(2,1)}, u32[]{:S(2)}, u32[]{:S(2)}) collective-permute-start(bf16[128,4096]{1,0:T(8,128)(2,1)} %shard_map.128), channel_id=1, source_target_pairs={{0,112},{16,0},{32,16},{48,32},{64,48},{80,64},{96,80},{112,96},{1... | collective-permute-start | bytes 3145736 | tf_op jit(solution)/shard_map/ppermute | solution.py:21
  (27 other events, 94.7 us)

commit v3 on v2

--- a/solution.py
+++ b/solution.py
@@ -73,7 +73,8 @@
     return lax.rsqrt(total * (1.0 / width) + epsilon)
 
 
-def normed_kernel(routes_ref, tokens_ref, norm_ref, out_ref, picks_ref, inv_rms_ref):
+def normed_kernel(routes_ref, *refs):
+    parts, (norm_ref, out_ref, picks_ref, inv_rms_ref) = refs[:4], refs[4:]
     experts, _, capacity, quarter = out_ref.shape
     q = pl.program_id(0)
 
@@ -81,14 +82,21 @@
     def _():
         for e, pick in enumerate(selections(routes_ref[...], experts, capacity)):
             picks_ref[e] = pick
-        inv_rms_ref[...] = inverse_rms(tokens_ref, quarter)
-
-    columns = pl.ds(pl.multiple_of(q * quarter, 128), quarter)
-    values = tokens_ref[:, columns].astype(jnp.float32)
-    norm = norm_ref[:, columns].astype(jnp.float32)
-    normed = (values * inv_rms_ref[...] * norm).astype(jnp.bfloat16)
-    for e in range(experts):
-        out_ref[e, 0] = contract(picks_ref[e], normed, 1, 0).astype(jnp.bfloat16)
+        total = 0.0
+        for part in parts:
+            values = part[...].astype(jnp.float32)
+            total = total + jnp.sum(values * values, axis=1, keepdims=True)
+        inv_rms_ref[...] = lax.rsqrt(total * (1.0 / (4 * quarter)) + epsilon)
+
+    for k, part in enumerate(parts):
+
+        @pl.when(q == k)
+        def _(k=k, part=part):
+            norm = norm_ref[:, k * quarter : (k + 1) * quarter].astype(jnp.float32)
+            values = part[...].astype(jnp.float32)
+            normed = (values * inv_rms_ref[...] * norm).astype(jnp.bfloat16)
+            for e in range(experts):
+                out_ref[e, 0] = contract(picks_ref[e], normed, 1, 0).astype(jnp.bfloat16)
 
 
 def scaled_kernel(routes_ref, weight_ref, grad_ref, out_ref):
@@ -121,8 +129,12 @@
     tok_count, width = tokens.shape
     return to_experts(
         normed_kernel,
-        (routes, tokens, norm),
-        [whole_block(routes), whole_block(tokens), whole_block(norm)],
+        (routes, *[tokens] * 4, norm),
+        [
+            whole_block(routes),
+            *[pl.BlockSpec((tok_count, width // 4), lambda q, k=k: (0, k)) for k in range(4)],
+            whole_block(norm),
+        ],
         experts,
         capacity,
         width // 4,

time: 306 us -> 307 us (level)
    unnamed x60 -> x64, local copies, waits for them, and re-layouts: 8.36 us -> 8.68 us
where the time goes in v3:
time: 307 us; the launch traced here: 306 us
  waiting for transfers between devices  153 us (50%)
  starting transfers between devices  61.7 us (20%)
  matrix products  39.8 us (13%)
  Pallas kernels  30 us (10%)
  other arithmetic  11.8 us (4%)
  local copies, waits for them, and re-layouts  8.93 us (3%)
    ppermute x12, waiting for transfers between devices, from_partner(): lax.ppermute(value, axis, [(i, i ^ 1 << bit) for i in range(lax.axis_size...  77.3 us
    all_to_all x6, waiting for transfers between devices, exchange(): return lax.all_to_all(value, 'ep', split_axis=0, concat_axis=0, tiled=True)  47.3 us
    dot_general x10, matrix products, contract(): lax.dot_general(left, right, (((left_dim,), (right_dim,)), ((), ())), pre...  39.8 us
    all_to_all x6, starting transfers between devices, exchange(): return lax.all_to_all(value, 'ep', split_axis=0, concat_axis=0, tiled=True)  31.6 us
    ppermute x3, waiting for transfers between devices, passed_along(): lax.ppermute(value, axis, [(i, (i + by) % count) for i in range(count)])  28.1 us
    ppermute x12, starting transfers between devices, from_partner(): lax.ppermute(value, axis, [(i, i ^ 1 << bit) for i in range(lax.axis_size...  18.2 us
    pallas_call x3, Pallas kernels, to_experts(): pl.pallas_call(kernel, out_shape=jax.ShapeDtypeStruct((experts, 4, capaci...  15 us
    pallas_call x6, Pallas kernels, local_call(): pl.pallas_call(kernel, out_shape=shapes, in_specs=[whole] * len(arrays),...  15 us
  transfers between devices with their start and end apart: 21, of which 14 were waited for; matrix products, arithmetic and copies ran while one was open for 14% of the time, Pallas kernels for 7%

profile of v3, /device:TPU:1, one launch (start us, length us, event | category | flops | bytes accessed | tf_op | source)
XLA Modules:
  0.0 306.0 jit_solution(6691730372509027260)
XLA Ops:
  0.6 5.1 %shard_map.122 = bf16[4,4,40,1792]{3,2,1,0:T(8,128)(2,1)} custom-call(s32[1,128]{1,0:T(1,128)} %bitcast.112, bf16[128,7168]{1,0:T(8,128)(2,1)} %bitcast.100, bf16[128,7168]{1,0:T(8,128)(2,1)} %bitcast.101, bf16[128,7168]{1,0:T(8,128)(2,1)} %bitcast.102, bf16[128,7168]{1,0:T(8,128)(2,1)} %bitcast.103, bf16[1,7168]{1,0:T(2,128)(2,1)} %norm_ref.3), custom_call_target="tpu_custom_call" | custom-call | flops 536870912 | bytes 8388608 | tf_op jit(solution)/shard_map/pallas_call | solution.py:112
  5.7 6.9 %all-to-all-start = ((bf16[16,40,1792]{2,1,0:T(8,128)(2,1)}), bf16[16,40,1792]{2,1,0:T(8,128)(2,1)S(1)}, u32[]{:S(2)}, u32[]{:S(2)}) async-start(bf16[16,40,1792]{2,1,0:T(8,128)(2,1)} %bitcast.115), calls=%async_computation | async-start | bytes 4587520 | tf_op jit(solution)/shard_map/all_to_all | solution.py:25
  12.6 5.1 %shard_map.123 = bf16[4,4,40,1792]{3,2,1,0:T(8,128)(2,1)} custom-call(s32[1,128]{1,0:T(1,128)} %bitcast.108, bf16[128,7168]{1,0:T(8,128)(2,1)} %bitcast.94, bf16[128,7168]{1,0:T(8,128)(2,1)} %bitcast.95, bf16[128,7168]{1,0:T(8,128)(2,1)} %bitcast.96, bf16[128,7168]{1,0:T(8,128)(2,1)} %bitcast.97, bf16[1,7168]{1,0:T(2,128)(2,1)} %norm_ref.3), custom_call_target="tpu_custom_call" | custom-call | flops 536870912 | bytes 8388608 | tf_op jit(solution)/shard_map/pallas_call | solution.py:112
  17.7 25.0 %all-to-all-done = bf16[16,40,1792]{2,1,0:T(8,128)(2,1)S(1)} async-done(((bf16[16,40,1792]{2,1,0:T(8,128)(2,1)}), bf16[16,40,1792]{2,1,0:T(8,128)(2,1)S(1)}, u32[]{:S(2)}, u32[]{:S(2)}) %all-to-all-start) | async-done | bytes 2293792 | tf_op jit(solution)/shard_map/all_to_all | solution.py:25
  42.7 7.1 %all-to-all-start.1 = ((bf16[16,40,1792]{2,1,0:T(8,128)(2,1)}), bf16[16,40,1792]{2,1,0:T(8,128)(2,1)}, u32[]{:S(2)}, u32[]{:S(2)}) async-start(bf16[16,40,1792]{2,1,0:T(8,128)(2,1)} %bitcast.114), calls=%async_computation.1 | async-start | bytes 4587520 | tf_op jit(solution)/shard_map/all_to_all | solution.py:25
  49.9 4.7 %fusion.23 = bf16[640,1024]{1,0:T(8,128)(2,1)S(1)} fusion(bf16[640,1792]{1,0:T(8,128)(2,1)S(1)} %bitcast.118, bf16[1,1,1792,1024]{3,2,1,0:T(8,128)(2,1)} %param.19), kind=kOutput, calls=%fused_computation.28 | convolution fusion | flops 2349465600 | bytes 7274496 | tf_op jit(solution)/shard_map/dot_general | solution.py:33
  60.2 4.8 %shard_map.124 = bf16[4,4,40,1792]{3,2,1,0:T(8,128)(2,1)} custom-call(s32[1,128]{1,0:T(1,128)} %bitcast.109, f32[1,128]{1,0:T(1,128)} %weight_ref.2, bf16[128,7168]{1,0:T(8,128)(2,1)} %bitcast.105), custom_call_target="tpu_custom_call" | custom-call | flops 536870912 | bytes 8388608 | tf_op jit(solution)/shard_map/pallas_call | solution.py:112
  65.3 28.1 %collective-permute-done.1 = bf16[320,1024]{1,0:T(8,128)(2,1)} collective-permute-done((bf16[320,1024]{1,0:T(8,128)(2,1)S(1)}, bf16[320,1024]{1,0:T(8,128)(2,1)}, u32[]{:S(2)}, u32[]{:S(2)}) %collective-permute-start.1) | collective-permute-done | bytes 655392 | tf_op jit(solution)/shard_map/ppermute | solution.py:16
  93.5 5.3 %fusion.26 = bf16[640,1024]{1,0:T(8,128)(2,1)S(1)} fusion(bf16[640,1792]{1,0:T(8,128)(2,1)} %bitcast.11, bf16[1,1,1792,1024]{3,2,1,0:T(8,128)(2,1)} %param.19), kind=kOutput, calls=%fused_computation.29 | convolution fusion | flops 2349465600 | bytes 7274496 | tf_op jit(solution)/shard_map/dot_general | solution.py:33
  101.5 4.4 %all-to-all-start.2 = ((bf16[16,40,1792]{2,1,0:T(8,128)(2,1)}), bf16[16,40,1792]{2,1,0:T(8,128)(2,1)}, u32[]{:S(2)}, u32[]{:S(2)}) async-start(bf16[16,40,1792]{2,1,0:T(8,128)(2,1)} %bitcast.24), calls=%async_computation.2 | async-start | bytes 4587520 | tf_op jit(solution)/shard_map/all_to_all | solution.py:25
  107.4 5.5 %fusion.32 = bf16[640,1024]{1,0:T(8,128)(2,1)S(1)} fusion(bf16[640,1792]{1,0:T(8,128)(2,1)} %bitcast.11, bf16[1,1,1792,1024]{3,2,1,0:T(8,128)(2,1)} %param.20), kind=kOutput, calls=%fused_computation.31 | convolution fusion | flops 2349465600 | bytes 7274496 | tf_op jit(solution)/shard_map/dot_general | solution.py:33
  120.4 28.7 %collective-permute-done.7 = bf16[320,1024]{1,0:T(8,128)(2,1)S(1)} collective-permute-done((bf16[320,1024]{1,0:T(8,128)(2,1)S(1)}, bf16[320,1024]{1,0:T(8,128)(2,1)S(1)}, u32[]{:S(2)}, u32[]{:S(2)}) %collective-permute-start.7) | collective-permute-done | bytes 655392 | tf_op jit(solution)/shard_map/ppermute | solution.py:16
  149.2 5.6 %fusion.35 = bf16[640,1024]{1,0:T(8,128)(2,1)S(1)} fusion(bf16[640,1792]{1,0:T(8,128)(2,1)} %bitcast.26, bf16[1,1,1024,1792]{3,2,1,0:T(8,128)(2,1)} %param.21), kind=kOutput, calls=%fused_computation.32 | convolution fusion | flops 2349465600 | bytes 7274496 | tf_op jit(solution)/shard_map/dot_general | solution.py:33
  163.4 4.9 %all-to-all-start.3 = ((bf16[16,40,1792]{2,1,0:T(8,128)(2,1)}), bf16[16,40,1792]{2,1,0:T(8,128)(2,1)S(1)}, u32[]{:S(2)}, u32[]{:S(2)}) async-start(bf16[16,40,1792]{2,1,0:T(8,128)(2,1)} %bitcast.117), calls=%async_computation.3 | async-start | bytes 4587520 | tf_op jit(solution)/shard_map/all_to_all | solution.py:25
  168.3 14.7 %collective-permute-done.10 = bf16[320,1024]{1,0:T(8,128)(2,1)} collective-permute-done((bf16[320,1024]{1,0:T(8,128)(2,1)S(1)}, bf16[320,1024]{1,0:T(8,128)(2,1)}, u32[]{:S(2)}, u32[]{:S(2)}) %collective-permute-start.10) | collective-permute-done | bytes 655392 | tf_op jit(solution)/shard_map/ppermute | solution.py:16
  187.6 9.5 %collective-permute-start.11 = (bf16[320,2176]{1,0:T(8,128)(2,1)}, bf16[320,2176]{1,0:T(8,128)(2,1)}, u32[]{:S(2)}, u32[]{:S(2)}) collective-permute-start(bf16[320,2176]{1,0:T(8,128)(2,1)} %pad_maximum_fusion), channel_id=1, source_target_pairs={{0,1},{1,0},{2,3},{3,2},{4,5},{5,4},{6,7},{7,6},{8,9},{9,8},{10,11... | collective-permute-start | bytes 4177928 | tf_op jit(solution)/shard_map/ppermute | solution.py:16
  197.1 8.8 %all-to-all-done.3.returned_ref = bf16[16,40,1792]{2,1,0:T(8,128)(2,1)S(1)} async-done(((bf16[16,40,1792]{2,1,0:T(8,128)(2,1)}), bf16[16,40,1792]{2,1,0:T(8,128)(2,1)S(1)}, u32[]{:S(2)}, u32[]{:S(2)}) %all-to-all-start.3) | async-done | bytes 2293792 | tf_op jit(solution)/shard_map/all_to_all | solution.py:25
  231.3 5.9 %all-to-all-done.4.returned_ref = bf16[16,40,896]{2,1,0:T(8,128)(2,1)S(1)} async-done(((bf16[16,40,896]{2,1,0:T(8,128)(2,1)}), bf16[16,40,896]{2,1,0:T(8,128)(2,1)S(1)}, u32[]{:S(2)}, u32[]{:S(2)}) %all-to-all-start.4) | async-done | bytes 1146912 | tf_op jit(solution)/shard_map/all_to_all | solution.py:25
  238.2 4.4 %all-to-all-start.5 = ((bf16[16,40,1024]{2,1,0:T(8,128)(2,1)}), bf16[16,40,1024]{2,1,0:T(8,128)(2,1)S(1)}, u32[]{:S(2)}, u32[]{:S(2)}) async-start(bf16[16,40,1024]{2,1,0:T(8,128)(2,1)} %bitcast.124), calls=%async_computation.5 | async-start | bytes 2621440 | tf_op jit(solution)/shard_map/all_to_all | solution.py:25
  247.8 5.9 %collective-permute-start.13 = (bf16[128,3072]{1,0:T(8,128)(2,1)}, bf16[128,3072]{1,0:T(8,128)(2,1)}, u32[]{:S(2)}, u32[]{:S(2)}) collective-permute-start(bf16[128,3072]{1,0:T(8,128)(2,1)} %get-tuple-element.26), channel_id=1, source_target_pairs={{0,112},{16,0},{32,16},{48,32},{64,48},{80,64},{96,80},{112,96},{1... | collective-permute-start | bytes 2359304 | tf_op jit(solution)/shard_map/ppermute | solution.py:21
  253.7 7.6 %all-to-all-done.5.returned_ref = bf16[16,40,1024]{2,1,0:T(8,128)(2,1)S(1)} async-done(((bf16[16,40,1024]{2,1,0:T(8,128)(2,1)}), bf16[16,40,1024]{2,1,0:T(8,128)(2,1)S(1)}, u32[]{:S(2)}, u32[]{:S(2)}) %all-to-all-start.5) | async-done | bytes 1310752 | tf_op jit(solution)/shard_map/all_to_all | solution.py:25
  265.3 6.0 %collective-permute-start.14 = (bf16[128,4096]{1,0:T(8,128)(2,1)}, bf16[128,4096]{1,0:T(8,128)(2,1)}, u32[]{:S(2)}, u32[]{:S(2)}) collective-permute-start(bf16[128,4096]{1,0:T(8,128)(2,1)} %shard_map.128), channel_id=1, source_target_pairs={{0,112},{16,0},{32,16},{48,32},{64,48},{80,64},{96,80},{112,96},{1... | collective-permute-start | bytes 3145736 | tf_op jit(solution)/shard_map/ppermute | solution.py:21
  275.2 21.3 %collective-permute-done.14.second_ref = bf16[128,4096]{1,0:T(8,128)(2,1)} collective-permute-done((bf16[128,4096]{1,0:T(8,128)(2,1)}, bf16[128,4096]{1,0:T(8,128)(2,1)}, u32[]{:S(2)}, u32[]{:S(2)}) %collective-permute-start.14) | collective-permute-done | bytes 1048608 | tf_op jit(solution)/shard_map/ppermute | solution.py:21
  299.1 4.1 %collective-permute-done.12.piece_ref = bf16[128,7168]{1,0:T(8,128)(2,1)} collective-permute-done((bf16[128,7168]{1,0:T(8,128)(2,1)}, bf16[128,7168]{1,0:T(8,128)(2,1)}, u32[]{:S(2)}, u32[]{:S(2)}) %collective-permute-start.12) | collective-permute-done | bytes 1835040 | tf_op jit(solution)/shard_map/ppermute | solution.py:21
  (120 shorter events, 75.5 us)
Async XLA Ops:
  5.7 37.0 %all-to-all-start = ((bf16[16,40,1792]{2,1,0:T(8,128)(2,1)}), bf16[16,40,1792]{2,1,0:T(8,128)(2,1)S(1)}, u32[]{:S(2)}, u32[]{:S(2)}) async-start(bf16[16,40,1792]{2,1,0:T(8,128)(2,1)} %bitcast.115), calls=%async_computation | async-start | bytes 4587520 | tf_op jit(solution)/shard_map/all_to_all | solution.py:25
  42.7 50.7 %all-to-all-start.1 = ((bf16[16,40,1792]{2,1,0:T(8,128)(2,1)}), bf16[16,40,1792]{2,1,0:T(8,128)(2,1)}, u32[]{:S(2)}, u32[]{:S(2)}) async-start(bf16[16,40,1792]{2,1,0:T(8,128)(2,1)} %bitcast.114), calls=%async_computation.1 | async-start | bytes 4587520 | tf_op jit(solution)/shard_map/all_to_all | solution.py:25
  54.7 3.4 %collective-permute-start = (bf16[320,1024]{1,0:T(8,128)(2,1)S(1)}, bf16[320,1024]{1,0:T(8,128)(2,1)S(1)}, u32[]{:S(2)}, u32[]{:S(2)}) collective-permute-start(bf16[320,1024]{1,0:T(8,128)(2,1)S(1)} %dynamic-slice_bitcast_fusion.4), channel_id=1, source_target_pairs={{0,1},{1,0},{2,3},{3,2},{4,5},{5,4},{6,7},{7,6},{8,9},{9,8},{10,11... | collective-permute-start | bytes 1966088 | tf_op jit(solution)/shard_map/ppermute | solution.py:16
  57.6 7.4 %collective-permute-start.3 = (bf16[320,1024]{1,0:T(8,128)(2,1)S(1)}, bf16[320,1024]{1,0:T(8,128)(2,1)S(1)}, u32[]{:S(2)}, u32[]{:S(2)}) collective-permute-start(bf16[320,1024]{1,0:T(8,128)(2,1)S(1)} %dynamic-slice_bitcast_fusion.2), channel_id=1, source_target_pairs={{0,1},{1,0},{2,3},{3,2},{4,5},{5,4},{6,7},{7,6},{8,9},{9,8},{10,11... | collective-permute-start | bytes 1966088 | tf_op jit(solution)/shard_map/ppermute | solution.py:16
  58.6 34.9 %collective-permute-start.1 = (bf16[320,1024]{1,0:T(8,128)(2,1)S(1)}, bf16[320,1024]{1,0:T(8,128)(2,1)}, u32[]{:S(2)}, u32[]{:S(2)}) collective-permute-start(bf16[320,1024]{1,0:T(8,128)(2,1)S(1)} %fusion.57), channel_id=1, source_target_pairs={{0,2},{1,3},{2,0},{3,1},{4,6},{5,7},{6,4},{7,5},{8,10},{9,11},{10,... | collective-permute-start | bytes 1966088 | tf_op jit(solution)/shard_map/ppermute | solution.py:16
  65.3 42.2 %collective-permute-start.4 = (bf16[320,1024]{1,0:T(8,128)(2,1)S(1)}, bf16[320,1024]{1,0:T(8,128)(2,1)S(1)}, u32[]{:S(2)}, u32[]{:S(2)}) collective-permute-start(bf16[320,1024]{1,0:T(8,128)(2,1)S(1)} %fusion.55), channel_id=1, source_target_pairs={{0,2},{1,3},{2,0},{3,1},{4,6},{5,7},{6,4},{7,5},{8,10},{9,11},{10,... | collective-permute-start | bytes 1966088 | tf_op jit(solution)/shard_map/ppermute | solution.py:16
  99.9 14.1 %collective-permute-start.2 = (bf16[320,1024]{1,0:T(8,128)(2,1)S(1)}, bf16[320,1024]{1,0:T(8,128)(2,1)S(1)}, u32[]{:S(2)}, u32[]{:S(2)}) collective-permute-start(bf16[320,1024]{1,0:T(8,128)(2,1)S(1)} %dynamic-slice_bitcast_fusion.3), channel_id=1, source_target_pairs={{0,1},{1,0},{2,3},{3,2},{4,5},{5,4},{6,7},{7,6},{8,9},{9,8},{10,11... | collective-permute-start | bytes 1966088 | tf_op jit(solution)/shard_map/ppermute | solution.py:16
  101.5 47.7 %all-to-all-start.2 = ((bf16[16,40,1792]{2,1,0:T(8,128)(2,1)}), bf16[16,40,1792]{2,1,0:T(8,128)(2,1)}, u32[]{:S(2)}, u32[]{:S(2)}) async-start(bf16[16,40,1792]{2,1,0:T(8,128)(2,1)} %bitcast.24), calls=%async_computation.2 | async-start | bytes 4587520 | tf_op jit(solution)/shard_map/all_to_all | solution.py:25
  113.0 2.7 collective-permute-start.5
  117.9 2.6 collective-permute-start.6
  118.7 30.5 %collective-permute-start.7 = (bf16[320,1024]{1,0:T(8,128)(2,1)S(1)}, bf16[320,1024]{1,0:T(8,128)(2,1)S(1)}, u32[]{:S(2)}, u32[]{:S(2)}) collective-permute-start(bf16[320,1024]{1,0:T(8,128)(2,1)S(1)} %fusion.56), channel_id=1, source_target_pairs={{0,2},{1,3},{2,0},{3,1},{4,6},{5,7},{6,4},{7,5},{8,10},{9,11},{10,... | collective-permute-start | bytes 1966088 | tf_op jit(solution)/shard_map/ppermute | solution.py:16
  118.7 44.6 %collective-permute-start.9 = (bf16[320,1024]{1,0:T(8,128)(2,1)S(1)}, bf16[320,1024]{1,0:T(8,128)(2,1)}, u32[]{:S(2)}, u32[]{:S(2)}) collective-permute-start(bf16[320,1024]{1,0:T(8,128)(2,1)S(1)} %fusion.54), channel_id=1, source_target_pairs={{0,2},{1,3},{2,0},{3,1},{4,6},{5,7},{6,4},{7,5},{8,10},{9,11},{10,... | collective-permute-start | bytes 1966088 | tf_op jit(solution)/shard_map/ppermute | solution.py:16
  120.4 34.3 %copy-start.27 = (bf16[320,1024]{1,0:T(8,128)(2,1)}, bf16[320,1024]{1,0:T(8,128)(2,1)S(1)}, u32[]{:S(2)}) copy-start(bf16[320,1024]{1,0:T(8,128)(2,1)S(1)} %collective-permute-done.6) | copy-start | bytes 1966084
  154.9 5.5 %collective-permute-start.8 = (bf16[320,1024]{1,0:T(8,128)(2,1)S(1)}, bf16[320,1024]{1,0:T(8,128)(2,1)S(1)}, u32[]{:S(2)}, u32[]{:S(2)}) collective-permute-start(bf16[320,1024]{1,0:T(8,128)(2,1)S(1)} %dynamic-slice_bitcast_fusion), channel_id=1, source_target_pairs={{0,1},{1,0},{2,3},{3,2},{4,5},{5,4},{6,7},{7,6},{8,9},{9,8},{10,11... | collective-permute-start | bytes 1966088 | tf_op jit(solution)/shard_map/ppermute | solution.py:16
  163.3 19.6 %collective-permute-start.10 = (bf16[320,1024]{1,0:T(8,128)(2,1)S(1)}, bf16[320,1024]{1,0:T(8,128)(2,1)}, u32[]{:S(2)}, u32[]{:S(2)}) collective-permute-start(bf16[320,1024]{1,0:T(8,128)(2,1)S(1)} %fusion.53), channel_id=1, source_target_pairs={{0,2},{1,3},{2,0},{3,1},{4,6},{5,7},{6,4},{7,5},{8,10},{9,11},{10,... | collective-permute-start | bytes 1966088 | tf_op jit(solution)/shard_map/ppermute | solution.py:16
  163.4 42.6 %all-to-all-start.3 = ((bf16[16,40,1792]{2,1,0:T(8,128)(2,1)}), bf16[16,40,1792]{2,1,0:T(8,128)(2,1)S(1)}, u32[]{:S(2)}, u32[]{:S(2)}) async-start(bf16[16,40,1792]{2,1,0:T(8,128)(2,1)} %bitcast.117), calls=%async_computation.3 | async-start | bytes 4587520 | tf_op jit(solution)/shard_map/all_to_all | solution.py:25
  187.6 18.4 %collective-permute-start.11 = (bf16[320,2176]{1,0:T(8,128)(2,1)}, bf16[320,2176]{1,0:T(8,128)(2,1)}, u32[]{:S(2)}, u32[]{:S(2)}) collective-permute-start(bf16[320,2176]{1,0:T(8,128)(2,1)} %pad_maximum_fusion), channel_id=1, source_target_pairs={{0,1},{1,0},{2,3},{3,2},{4,5},{5,4},{6,7},{7,6},{8,9},{9,8},{10,11... | collective-permute-start | bytes 4177928 | tf_op jit(solution)/shard_map/ppermute | solution.py:16
  216.3 20.8 %all-to-all-start.4 = ((bf16[16,40,896]{2,1,0:T(8,128)(2,1)}), bf16[16,40,896]{2,1,0:T(8,128)(2,1)S(1)}, u32[]{:S(2)}, u32[]{:S(2)}) async-start(bf16[16,40,896]{2,1,0:T(8,128)(2,1)} %bitcast.116), calls=%async_computation.4 | async-start | bytes 2293760 | tf_op jit(solution)/shard_map/all_to_all | solution.py:25
  231.3 11.3 %copy-start.8 = (bf16[1,7168]{1,0:T(2,128)(2,1)S(1)}, bf16[1,7168]{1,0:T(2,128)(2,1)}, u32[]{:S(2)}) copy-start(bf16[1,7168]{1,0:T(2,128)(2,1)} %norm_ref.3) | copy-start | bytes 43012
  231.3 11.3 %copy-start.9 = (s32[1,128,1]{1,2,0:T(1,128)S(1)}, s32[1,128,1]{1,2,0:T(1,128)}, u32[]{:S(2)}) copy-start(s32[1,128,1]{1,2,0:T(1,128)} %param.16) | copy-start | bytes 1540
  238.2 23.1 %all-to-all-start.5 = ((bf16[16,40,1024]{2,1,0:T(8,128)(2,1)}), bf16[16,40,1024]{2,1,0:T(8,128)(2,1)S(1)}, u32[]{:S(2)}, u32[]{:S(2)}) async-start(bf16[16,40,1024]{2,1,0:T(8,128)(2,1)} %bitcast.124), calls=%async_computation.5 | async-start | bytes 2621440 | tf_op jit(solution)/shard_map/all_to_all | solution.py:25
  247.8 26.3 %collective-permute-start.13 = (bf16[128,3072]{1,0:T(8,128)(2,1)}, bf16[128,3072]{1,0:T(8,128)(2,1)}, u32[]{:S(2)}, u32[]{:S(2)}) collective-permute-start(bf16[128,3072]{1,0:T(8,128)(2,1)} %get-tuple-element.26), channel_id=1, source_target_pairs={{0,112},{16,0},{32,16},{48,32},{64,48},{80,64},{96,80},{112,96},{1... | collective-permute-start | bytes 2359304 | tf_op jit(solution)/shard_map/ppermute | solution.py:21
  253.7 49.5 %collective-permute-start.12 = (bf16[128,7168]{1,0:T(8,128)(2,1)}, bf16[128,7168]{1,0:T(8,128)(2,1)}, u32[]{:S(2)}, u32[]{:S(2)}) collective-permute-start(bf16[128,7168]{1,0:T(8,128)(2,1)} %shard_map.125), channel_id=1, source_target_pairs={{0,16},{16,32},{32,48},{48,64},{64,80},{80,96},{96,112},{112,0},{1... | collective-permute-start | bytes 5505032 | tf_op jit(solution)/shard_map/ppermute | solution.py:21
  265.3 31.2 %collective-permute-start.14 = (bf16[128,4096]{1,0:T(8,128)(2,1)}, bf16[128,4096]{1,0:T(8,128)(2,1)}, u32[]{:S(2)}, u32[]{:S(2)}) collective-permute-start(bf16[128,4096]{1,0:T(8,128)(2,1)} %shard_map.128), channel_id=1, source_target_pairs={{0,112},{16,0},{32,16},{48,32},{64,48},{80,64},{96,80},{112,96},{1... | collective-permute-start | bytes 3145736 | tf_op jit(solution)/shard_map/ppermute | solution.py:21
  (29 other events, 101.3 us)
